TPU v7x, 32 devices: a whole 2x2x4 slice. The times are simulated.
32 devices in a mesh: dp: 8 (over z, y), tensor: 4 (over x, core).
Axes of the slice: x: 2, y: 2, z: 4, core: 2. Of those that a mesh axis runs over, the one named last changes fastest.
Arguments:
- tokens: bfloat16 [16384, 1024], P(('dp', 'tensor')), may hold values from -6 to 6
- out_grad: bfloat16 [16384, 1024], P(('dp', 'tensor')), may hold values from -6 to 6
- seq_lengths: int32 [8, 4], P('dp'), may hold values from 1 to 1536, as said below
- norm1_gain: float32 [1024], P(('dp', 'tensor')), may hold values from 0.5 to 1.5
- norm1_bias: float32 [1024], P(('dp', 'tensor')), may hold values from -1.25 to 1.25
- norm2_gain: float32 [1024], P(('dp', 'tensor')), may hold values from 0.5 to 1.5
- norm2_bias: float32 [1024], P(('dp', 'tensor')), may hold values from -1.25 to 1.25
- w_query: bfloat16 [1024, 1024], P('dp', 'tensor'), may hold values from -0.1875 to 0.1875
- b_query: float32 [1024], P(('dp', 'tensor')), may hold values from -1.25 to 1.25
- w_key: bfloat16 [1024, 1024], P('dp', 'tensor'), may hold values from -0.1875 to 0.1875
- b_key: float32 [1024], P(('dp', 'tensor')), may hold values from -1.25 to 1.25
- w_value: bfloat16 [1024, 1024], P('dp', 'tensor'), may hold values from -0.1875 to 0.1875
- b_value: float32 [1024], P(('dp', 'tensor')), may hold values from -1.25 to 1.25
- w_dense: bfloat16 [1024, 1024], P('tensor', 'dp'), may hold values from -3 to 3
- b_dense: float32 [1024], P(('dp', 'tensor')), may hold values from -1.25 to 1.25
- w_up: bfloat16 [1024, 4096], P('dp', 'tensor'), may hold values from -0.1875 to 0.1875
- b_up: float32 [4096], P(('dp', 'tensor')), may hold values from -1.25 to 1.25
- w_down: bfloat16 [4096, 1024], P('tensor', 'dp'), may hold values from -0.09375 to 0.09375
- b_down: float32 [1024], P(('dp', 'tensor')), may hold values from -1.25 to 1.25
Outputs:
- layer_out: bfloat16 [16384, 1024], P(('dp', 'tensor'))
- tokens_grad: float32 [16384, 1024], P(('dp', 'tensor'))
- grad_norm1_gain: float32 [1024], P(('dp', 'tensor'))
- grad_norm1_bias: float32 [1024], P(('dp', 'tensor'))
- grad_norm2_gain: float32 [1024], P(('dp', 'tensor'))
- grad_norm2_bias: float32 [1024], P(('dp', 'tensor'))
- grad_w_query: float32 [1024, 1024], P('dp', 'tensor')
- grad_b_query: float32 [1024], P(('dp', 'tensor'))
- grad_w_key: float32 [1024, 1024], P('dp', 'tensor')
- grad_b_key: float32 [1024], P(('dp', 'tensor'))
- grad_w_value: float32 [1024, 1024], P('dp', 'tensor')
- grad_b_value: float32 [1024], P(('dp', 'tensor'))
- grad_w_dense: float32 [1024, 1024], P('tensor', 'dp')
- grad_b_dense: float32 [1024], P(('dp', 'tensor'))
- grad_w_up: float32 [1024, 4096], P('dp', 'tensor')
- grad_b_up: float32 [4096], P(('dp', 'tensor'))
- grad_w_down: float32 [4096, 1024], P('tensor', 'dp')
- grad_b_down: float32 [1024], P(('dp', 'tensor'))
Inputs may be any that keep to these rules, and one draw needn't show every extreme that they name: `seq_lengths`: each row gives the lengths of the 4 sequences packed in order into one group of 2048 tokens and sums to 2048. The second sequence of each row is exactly 1536 long and starts within the group's first 512 tokens; the other three together are 512 long.
All inputs are finite; a program needn't handle non-finite values.
Results may differ from a plain program's by a relative error of at most 0.01575.
Values may be sent and summed in bfloat16 or wider, within the bound.
A program may use at most 256 MiB of HBM per device.

v0:
```python
import math

import jax
import jax.numpy as jnp
from jax import lax
from jax.sharding import PartitionSpec as P

HEAD = 64
FF = 4096
ROTARY = 16
BLOCK = 512


EPS = 1e-05
MASKED_SCORE = -1e30


def layer_norm(row_vals, gain_vec, shift_vec):
    row_mean = jnp.mean(row_vals, axis=-1, keepdims=True)
    centred = row_vals - row_mean
    row_var = jnp.mean(centred * centred, axis=-1, keepdims=True)
    return centred * lax.rsqrt(row_var + EPS) * gain_vec + shift_vec


def smooth(values):
    return jax.nn.gelu(values, approximate=False)


def segment_rows(lengths, group_size):
    seq_ends = jnp.cumsum(lengths, dtype=jnp.int32)
    seq_starts = seq_ends - lengths
    row_index = jnp.arange(group_size, dtype=jnp.int32)
    segment = jnp.sum(
        (row_index[:, None] >= seq_ends[None, :]).astype(jnp.int32), axis=1, dtype=jnp.int32
    )
    seq_begin = jnp.max(
        jnp.where(row_index[:, None] >= seq_starts[None, :], seq_starts[None, :], 0), axis=1
    )
    return (row_index, segment, (row_index - seq_begin).astype(jnp.float32))


def rotary_tables(positions, rot_dims):
    half_rot = rot_dims // 2
    frequency = 10000.0 ** (-2.0 * jnp.arange(half_rot, dtype=jnp.float32) / rot_dims)
    angles = positions[:, None] * frequency[None, :]
    cosine_half = jnp.cos(angles)
    sine_half = jnp.sin(angles)
    return (
        jnp.concatenate([cosine_half, cosine_half], 1),
        jnp.concatenate([sine_half, sine_half], 1),
    )


def rotate(head_vals, cosine_table, sine_table):
    rot_dims = cosine_table.shape[1]
    half_rot = rot_dims // 2
    rot_part = head_vals[..., :rot_dims]
    turned = jnp.concatenate([-rot_part[..., half_rot:], rot_part[..., :half_rot]], -1)
    turned_part = rot_part * cosine_table[:, None, :] + turned * sine_table[:, None, :]
    return jnp.concatenate([turned_part, head_vals[..., rot_dims:]], -1)


def per_device(
    tokens,
    out_grad,
    seq_lengths,
    norm1_gain,
    norm1_bias,
    norm2_gain,
    norm2_bias,
    w_query,
    b_query,
    w_key,
    b_key,
    w_value,
    b_value,
    w_dense,
    b_dense,
    w_up,
    b_up,
    w_down,
    b_down,
):
    gathered_small = (
        lax.all_gather(norm1_gain, ("dp", "tensor"), axis=0, tiled=True),
        lax.all_gather(norm1_bias, ("dp", "tensor"), axis=0, tiled=True),
        lax.all_gather(norm2_gain, ("dp", "tensor"), axis=0, tiled=True),
        lax.all_gather(norm2_bias, ("dp", "tensor"), axis=0, tiled=True),
        lax.all_gather(b_query, ("dp", "tensor"), axis=0, tiled=True),
        lax.all_gather(b_key, ("dp", "tensor"), axis=0, tiled=True),
        lax.all_gather(b_value, ("dp", "tensor"), axis=0, tiled=True),
        lax.all_gather(b_dense, ("dp", "tensor"), axis=0, tiled=True),
        lax.all_gather(b_up, ("dp", "tensor"), axis=0, tiled=True),
        lax.all_gather(b_down, ("dp", "tensor"), axis=0, tiled=True),
    )
    (
        gain_one,
        shift_one,
        gain_two,
        shift_two,
        bias_query,
        bias_key,
        bias_value,
        bias_dense,
        bias_up,
        bias_down,
    ) = gathered_small
    width = tokens.shape[1]
    column_count = w_query.shape[1]
    hidden_count = w_up.shape[1]
    heads_here = column_count // HEAD
    tensor_at = lax.axis_index("tensor")
    bias_query = lax.dynamic_slice_in_dim(bias_query, tensor_at * column_count, column_count)
    bias_key = lax.dynamic_slice_in_dim(bias_key, tensor_at * column_count, column_count)
    bias_value = lax.dynamic_slice_in_dim(bias_value, tensor_at * column_count, column_count)
    bias_up = lax.dynamic_slice_in_dim(bias_up, tensor_at * hidden_count, hidden_count)
    own_rows = tokens.astype(jnp.float32)
    normed_one = layer_norm(own_rows, gain_one, shift_one).astype(jnp.bfloat16)
    normed_two = layer_norm(own_rows, gain_two, shift_two).astype(jnp.bfloat16)
    normed_one, normed_two = (
        lax.all_gather(normed_one, "tensor", axis=0, tiled=True),
        lax.all_gather(normed_two, "tensor", axis=0, tiled=True),
    )
    group_size = normed_one.shape[0]
    row_index, segment, positions = segment_rows(seq_lengths.reshape(-1), group_size)
    cosine_table, sine_table = rotary_tables(positions, ROTARY)
    score_scale = 1.0 / math.sqrt(HEAD)
    pieces = (
        lax.all_gather(w_query, "dp", axis=0, tiled=True),
        lax.all_gather(w_key, "dp", axis=0, tiled=True),
        lax.all_gather(w_value, "dp", axis=0, tiled=True),
        lax.all_gather(w_up, "dp", axis=0, tiled=True),
    )
    query_raw = jnp.dot(normed_one, pieces[0], preferred_element_type=jnp.float32)
    key_raw = jnp.dot(normed_one, pieces[1], preferred_element_type=jnp.float32)
    value_raw = jnp.dot(normed_one, pieces[2], preferred_element_type=jnp.float32)
    up_raw = jnp.dot(normed_two, pieces[3], preferred_element_type=jnp.float32)
    queries = rotate(
        (query_raw + bias_query).reshape(group_size, heads_here, HEAD), cosine_table, sine_table
    ).astype(jnp.bfloat16)
    key_heads = rotate(
        (key_raw + bias_key).reshape(group_size, heads_here, HEAD), cosine_table, sine_table
    ).astype(jnp.bfloat16)
    values = (value_raw + bias_value).astype(jnp.bfloat16).reshape(group_size, heads_here, HEAD)
    block_rows = min(BLOCK, group_size)
    block_count = group_size // block_rows
    context_parts = []
    logsum_parts = []
    for block_at in range(block_count):
        low_row = block_at * block_rows
        high_row = low_row + block_rows
        allowed = (segment[low_row:high_row, None] == segment[None, :high_row]) & (
            row_index[low_row:high_row, None] >= row_index[None, :high_row]
        )
        scores = (
            jnp.einsum(
                "qhd,khd->hqk",
                queries[low_row:high_row],
                key_heads[:high_row],
                preferred_element_type=jnp.float32,
            )
            * score_scale
        )
        scores = jnp.where(allowed[None], scores, MASKED_SCORE)
        row_peak = jnp.max(scores, axis=-1, keepdims=True)
        expd = jnp.exp(scores - row_peak)
        row_total = jnp.sum(expd, axis=-1, keepdims=True)
        attn_probs = (expd / row_total).astype(jnp.bfloat16)
        context_parts.append(
            jnp.einsum(
                "hqk,khd->qhd", attn_probs, values[:high_row], preferred_element_type=jnp.float32
            )
        )
        logsum_parts.append(row_peak + jnp.log(row_total))
    context = (
        jnp.concatenate(context_parts, 0).reshape(group_size, column_count).astype(jnp.bfloat16)
    )
    hidden_pre = up_raw + bias_up
    activated = smooth(hidden_pre).astype(jnp.bfloat16)
    pieces = (
        lax.all_gather(w_dense, "dp", axis=1, tiled=True),
        lax.all_gather(w_down, "dp", axis=1, tiled=True),
    )
    partial_cols = jnp.dot(context, pieces[0], preferred_element_type=jnp.float32)
    partial_cols = partial_cols + jnp.dot(activated, pieces[1], preferred_element_type=jnp.float32)
    summed = lax.psum_scatter(
        partial_cols.astype(jnp.bfloat16), "tensor", scatter_dimension=0, tiled=True
    ).astype(jnp.float32)
    layer_out = (own_rows + summed + bias_dense + bias_down).astype(jnp.bfloat16)
    grad_group = lax.all_gather(out_grad, "tensor", axis=0, tiled=True)
    grad_dense = jnp.einsum("gc,gd->cd", context, grad_group, preferred_element_type=jnp.float32)
    grad_down = jnp.einsum("gf,gd->fd", activated, grad_group, preferred_element_type=jnp.float32)
    grad_dense, grad_down = (
        lax.psum_scatter(grad_dense, "dp", scatter_dimension=1, tiled=True),
        lax.psum_scatter(grad_down, "dp", scatter_dimension=1, tiled=True),
    )
    pieces = (
        lax.all_gather(w_dense, "dp", axis=1, tiled=True),
        lax.all_gather(w_down, "dp", axis=1, tiled=True),
    )
    grad_context = jnp.einsum(
        "gd,cd->gc", grad_group, pieces[0], preferred_element_type=jnp.float32
    )
    grad_act = jnp.einsum("gd,fd->gf", grad_group, pieces[1], preferred_element_type=jnp.float32)
    grad_context = grad_context.astype(jnp.bfloat16).reshape(group_size, heads_here, HEAD)
    gelu_value, gelu_back = jax.vjp(smooth, hidden_pre)
    grad_hidden = gelu_back(grad_act)[0].astype(jnp.bfloat16)
    query_parts = []
    key_total = jnp.zeros((group_size, heads_here, HEAD), jnp.float32)
    value_total = jnp.zeros((group_size, heads_here, HEAD), jnp.float32)
    for block_at in range(block_count):
        low_row = block_at * block_rows
        high_row = low_row + block_rows
        allowed = (segment[low_row:high_row, None] == segment[None, :high_row]) & (
            row_index[low_row:high_row, None] >= row_index[None, :high_row]
        )
        query_blk = queries[low_row:high_row]
        scores = (
            jnp.einsum(
                "qhd,khd->hqk", query_blk, key_heads[:high_row], preferred_element_type=jnp.float32
            )
            * score_scale
        )
        scores = jnp.where(allowed[None], scores, MASKED_SCORE)
        probs_full = jnp.exp(scores - logsum_parts[block_at])
        grad_blk = grad_context[low_row:high_row]
        grad_probs = jnp.einsum(
            "qhd,khd->hqk", grad_blk, values[:high_row], preferred_element_type=jnp.float32
        )
        row_inner = jnp.sum(grad_probs * probs_full, axis=-1, keepdims=True)
        grad_scores = (probs_full * (grad_probs - row_inner)).astype(jnp.bfloat16)
        query_parts.append(
            jnp.einsum(
                "hqk,khd->qhd",
                grad_scores,
                key_heads[:high_row],
                preferred_element_type=jnp.float32,
            )
            * score_scale
        )
        key_total = key_total.at[:high_row].add(
            jnp.einsum("hqk,qhd->khd", grad_scores, query_blk, preferred_element_type=jnp.float32)
            * score_scale
        )
        value_total = value_total.at[:high_row].add(
            jnp.einsum(
                "hqk,qhd->khd",
                probs_full.astype(jnp.bfloat16),
                grad_blk,
                preferred_element_type=jnp.float32,
            )
        )
    rotated_zero, rotate_back = jax.vjp(
        lambda head_vals: rotate(head_vals, cosine_table, sine_table),
        jnp.zeros((group_size, heads_here, HEAD), jnp.float32),
    )
    grad_query = (
        rotate_back(jnp.concatenate(query_parts, 0))[0]
        .reshape(group_size, column_count)
        .astype(jnp.bfloat16)
    )
    grad_key = rotate_back(key_total)[0].reshape(group_size, column_count).astype(jnp.bfloat16)
    grad_value = value_total.reshape(group_size, column_count).astype(jnp.bfloat16)
    grad_wq = jnp.einsum("gd,gc->dc", normed_one, grad_query, preferred_element_type=jnp.float32)
    grad_wk = jnp.einsum("gd,gc->dc", normed_one, grad_key, preferred_element_type=jnp.float32)
    grad_wv = jnp.einsum("gd,gc->dc", normed_one, grad_value, preferred_element_type=jnp.float32)
    grad_wu = jnp.einsum("gd,gf->df", normed_two, grad_hidden, preferred_element_type=jnp.float32)
    grads_in = (
        lax.psum_scatter(grad_wq, "dp", scatter_dimension=0, tiled=True),
        lax.psum_scatter(grad_wk, "dp", scatter_dimension=0, tiled=True),
        lax.psum_scatter(grad_wv, "dp", scatter_dimension=0, tiled=True),
        lax.psum_scatter(grad_wu, "dp", scatter_dimension=0, tiled=True),
    )
    pieces = (
        lax.all_gather(w_query, "dp", axis=0, tiled=True),
        lax.all_gather(w_key, "dp", axis=0, tiled=True),
        lax.all_gather(w_value, "dp", axis=0, tiled=True),
        lax.all_gather(w_up, "dp", axis=0, tiled=True),
    )
    part_one = jnp.einsum("gc,dc->gd", grad_query, pieces[0], preferred_element_type=jnp.float32)
    part_one = part_one + jnp.einsum(
        "gc,dc->gd", grad_key, pieces[1], preferred_element_type=jnp.float32
    )
    part_one = part_one + jnp.einsum(
        "gc,dc->gd", grad_value, pieces[2], preferred_element_type=jnp.float32
    )
    part_two = jnp.einsum("gf,df->gd", grad_hidden, pieces[3], preferred_element_type=jnp.float32)
    share_one, share_two = (
        lax.psum_scatter(
            part_one.astype(jnp.bfloat16), "tensor", scatter_dimension=0, tiled=True
        ).astype(jnp.float32),
        lax.psum_scatter(
            part_two.astype(jnp.bfloat16), "tensor", scatter_dimension=0, tiled=True
        ).astype(jnp.float32),
    )
    normed_val_one, back_one = jax.vjp(layer_norm, own_rows, gain_one, shift_one)
    normed_val_two, back_two = jax.vjp(layer_norm, own_rows, gain_two, shift_two)
    input_one, d_gain_one, d_shift_one = back_one(share_one)
    input_two, d_gain_two, d_shift_two = back_two(share_two)
    tokens_grad = out_grad.astype(jnp.float32) + input_one + input_two

    def placed(vector, full_len):
        return lax.dynamic_update_slice_in_dim(
            jnp.zeros((full_len,), jnp.float32), vector, tensor_at * vector.shape[0], 0
        )

    bias_sum = jnp.sum(out_grad, axis=0, dtype=jnp.float32)
    small_grads = (
        lax.psum_scatter(d_gain_one, ("dp", "tensor"), scatter_dimension=0, tiled=True),
        lax.psum_scatter(d_shift_one, ("dp", "tensor"), scatter_dimension=0, tiled=True),
        lax.psum_scatter(d_gain_two, ("dp", "tensor"), scatter_dimension=0, tiled=True),
        lax.psum_scatter(d_shift_two, ("dp", "tensor"), scatter_dimension=0, tiled=True),
        lax.psum_scatter(
            placed(jnp.sum(grad_query, axis=0, dtype=jnp.float32), width),
            ("dp", "tensor"),
            scatter_dimension=0,
            tiled=True,
        ),
        lax.psum_scatter(
            placed(jnp.sum(grad_key, axis=0, dtype=jnp.float32), width),
            ("dp", "tensor"),
            scatter_dimension=0,
            tiled=True,
        ),
        lax.psum_scatter(
            placed(jnp.sum(grad_value, axis=0, dtype=jnp.float32), width),
            ("dp", "tensor"),
            scatter_dimension=0,
            tiled=True,
        ),
        lax.psum_scatter(bias_sum, ("dp", "tensor"), scatter_dimension=0, tiled=True),
        lax.psum_scatter(
            placed(jnp.sum(grad_hidden, axis=0, dtype=jnp.float32), FF),
            ("dp", "tensor"),
            scatter_dimension=0,
            tiled=True,
        ),
    )
    return (
        layer_out,
        tokens_grad,
        small_grads[0],
        small_grads[1],
        small_grads[2],
        small_grads[3],
        grads_in[0],
        small_grads[4],
        grads_in[1],
        small_grads[5],
        grads_in[2],
        small_grads[6],
        grad_dense,
        small_grads[7],
        grads_in[3],
        small_grads[8],
        grad_down,
        small_grads[7],
    )


def solution(mesh):
    in_specs = (
        P(("dp", "tensor"), None),
        P(("dp", "tensor"), None),
        P("dp", None),
        P(("dp", "tensor")),
        P(("dp", "tensor")),
        P(("dp", "tensor")),
        P(("dp", "tensor")),
        P("dp", "tensor"),
        P(("dp", "tensor")),
        P("dp", "tensor"),
        P(("dp", "tensor")),
        P("dp", "tensor"),
        P(("dp", "tensor")),
        P("tensor", "dp"),
        P(("dp", "tensor")),
        P("dp", "tensor"),
        P(("dp", "tensor")),
        P("tensor", "dp"),
        P(("dp", "tensor")),
    )
    out_specs = (
        P(("dp", "tensor"), None),
        P(("dp", "tensor"), None),
        P(("dp", "tensor")),
        P(("dp", "tensor")),
        P(("dp", "tensor")),
        P(("dp", "tensor")),
        P("dp", "tensor"),
        P(("dp", "tensor")),
        P("dp", "tensor"),
        P(("dp", "tensor")),
        P("dp", "tensor"),
        P(("dp", "tensor")),
        P("tensor", "dp"),
        P(("dp", "tensor")),
        P("dp", "tensor"),
        P(("dp", "tensor")),
        P("tensor", "dp"),
        P(("dp", "tensor")),
    )
    return jax.shard_map(
        per_device, mesh=mesh, in_specs=in_specs, out_specs=out_specs, check_vma=False
    )
```

profile of v0, /device:TPU:0, one launch (start us, length us, event | category | flops | bytes accessed | tf_op | source)
XLA Modules:
  0.0 986.0 jit_solution(17738280464801383465)
XLA Ops:
  16.3 42.4 %all-reduce.29 = (f32[1024]{0:T(1024)S(1)}, f32[1024]{0:T(1024)S(1)}, f32[1024]{0:T(1024)S(1)}, f32[1024]{0:T(1024)S(1)}, f32[1024]{0:T(1024)S(1)}, /*index=5*/f32[1024]{0:T(1024)S(1)}, f32[1024]{0:T(1024)S(1)}) all-reduce(f32[1024]{0:T(1024)S(1)} %dynamic-update-slice.28, ...), channel_id=1, replica_groups=mesh['dp'=8,'tensor'=4] {'dp','tensor'}, use_global_device_ids=true, to_apply=%add.16 | all-reduce | flops 7168 | bytes 57344
  65.5 40.0 %all-gather = f32[32,1,128]{2,1,0:T(1,128)S(1)} all-gather(f32[1,1,128]{2,1,0:T(1,128)S(1)} %bitcast.185), channel_id=1, replica_groups=mesh['dp'=8,'tensor'=4] {'dp','tensor'}, dimensions={0}, use_global_device_ids=true | all-gather | bytes 16896 | tf_op jit(solution)/shard_map/all_gather | solution.py:93
  105.5 33.4 %all_gather.68 = bf16[1024,256]{1,0:T(8,128)(2,1)} all-gather(bf16[128,256]{1,0:T(8,128)(2,1)S(1)} %copy-done.80), channel_id=1, replica_groups=mesh['dp'=8,'tensor'=4] {'dp'}, dimensions={0}, use_global_device_ids=true | all-gather | bytes 589824 | tf_op jit(solution)/shard_map/all_gather | solution.py:129
  139.0 31.9 %all_gather.70 = bf16[1024,256]{1,0:T(8,128)(2,1)S(1)} all-gather(bf16[128,256]{1,0:T(8,128)(2,1)S(1)} %copy-done.81), channel_id=1, replica_groups=mesh['dp'=8,'tensor'=4] {'dp'}, dimensions={0}, use_global_device_ids=true | all-gather | bytes 589824 | tf_op jit(solution)/shard_map/all_gather | solution.py:130
  170.9 32.0 %all_gather.66 = bf16[1024,256]{1,0:T(8,128)(2,1)S(1)} all-gather(bf16[128,256]{1,0:T(8,128)(2,1)S(1)} %copy-done.82), channel_id=1, replica_groups=mesh['dp'=8,'tensor'=4] {'dp'}, dimensions={0}, use_global_device_ids=true | all-gather | bytes 589824 | tf_op jit(solution)/shard_map/all_gather | solution.py:131
  203.0 27.2 %all_gather.72 = bf16[256,1024]{1,0:T(8,128)(2,1)S(1)} all-gather(bf16[256,128]{1,0:T(8,128)(2,1)S(1)} %copy-done.83), channel_id=1, replica_groups=mesh['dp'=8,'tensor'=4] {'dp'}, dimensions={1}, use_global_device_ids=true | all-gather | bytes 589824 | tf_op jit(solution)/shard_map/all_gather | solution.py:181
  294.8 10.7 %fusion.140 = f32[2048,1024]{1,0:T(8,128)} fusion(bf16[2048,1024]{1,0:T(8,128)(2,1)} %all-gather.9.cloned.1.call-done, bf16[1024,1024]{1,0:T(8,128)(2,1)} %all-gather.11.cloned.1.call-done), kind=kOutput, calls=%fused_computation.236 | convolution fusion | flops 4294967296 | bytes 14680064 | tf_op jit(solution)/shard_map/dot_general | solution.py:137
  305.6 28.4 %convert_reduce_fusion = (f32[1024]{0:T(1024)}, bf16[2048,1024]{1,0:T(8,128)(2,1)S(1)}, f32[2048,1024]{1,0:T(8,128)}) fusion(f32[2048,1024]{1,0:T(8,128)} %fusion.140, f32[1024]{0:T(1024)S(1)} %dynamic_slice.15, bf16[2048,1024]{1,0:T(8,128)(2,1)} %all-gather.15.cloned.1.call-done, bf16[1024,1024]{1,0:T(8,128)(2,1)} %all-gather.13.cloned.1.call-done), kind=kOutput, calls=%fused_computation.19 | convolution fusion | flops 4452252672 | bytes 27271168 | tf_op jit(solution)/shard_map/gd,fd->gf/dot_general | solution.py:204
  335.9 6.6 convolution_convert_fusion
  343.9 8.4 fusion.136
  352.3 8.8 fusion
  361.1 15.4 %multiply_reduce_fusion = (f32[4,512]{1,0:T(4,128)S(1)}, f32[4,512,2048]{2,1,0:T(8,128)}) fusion(f32[4,512,2048]{2,1,0:T(8,128)} %get-tuple-element.197, f32[4,512]{1,0:T(4,128)S(1)} %log_add_fusion, bf16[512,4,64]{0,2,1:T(8,128)(2,1)S(1)} %bitcast.163, bf16[2048,4,64]{0,2,1:T(8,128)(2,1)S(1)} %bitcast.153), kind=kOutput, calls=%fused_computation.1 | convolution fusion | flops 549451776 | bytes 34881536 | tf_op jit(solution)/shard_map/qhd,khd->hqk/dot_general | solution.py:227
  376.9 10.8 %multiply_convert_fusion = bf16[4,512,2048]{2,1,0:T(8,128)(2,1)} fusion(f32[4,512,2048]{2,1,0:T(8,128)} %get-tuple-element.199, f32[4,512,2048]{2,1,0:T(8,128)S(1)} %bitcast.144, f32[4,512]{1,0:T(4,128)S(1)} %get-tuple-element.198, f32[4,512]{1,0:T(4,128)S(1)} %log_add_fusion), kind=kLoop, calls=%fused_computation | loop fusion | flops 16777216 | bytes 41959424 | tf_op jit(solution)/shard_map/convert_element_type | solution.py:231
  429.8 9.1 add_convert_fusion.1
  461.5 10.3 %multiply_convert_fusion.3 = bf16[2048,1024]{1,0:T(8,128)(2,1)} fusion(f32[2048,1024]{1,0:T(8,128)} %get-tuple-element.160, f32[2048,1024]{1,0:T(8,128)} %fusion.140, f32[1024]{0:T(1024)S(1)} %dynamic_slice.15), kind=kLoop, calls=%fused_computation.27 | loop fusion | flops 8388608 | bytes 20975616 | tf_op jit(solution)/shard_map/convert_element_type | solution.py:179
  501.2 10.3 %fusion.148 = f32[1024,1024]{1,0:T(8,128)} fusion(bf16[2048,1024]{1,0:T(8,128)(2,1)} %all-gather.9.cloned.1.call-done, bf16[2048,1024]{1,0:T(8,128)(2,1)} %copy-done.105), kind=kOutput, calls=%fused_computation.244 | convolution fusion | flops 4294967296 | bytes 12582912 | tf_op jit(solution)/shard_map/gd,gf->df/dot_general | solution.py:267
  511.6 10.1 %fusion.149 = f32[1024,1024]{1,0:T(8,128)} fusion(bf16[2048,1024]{1,0:T(8,128)(2,1)} %multiply_convert_fusion.3, bf16[2048,1024]{1,0:T(8,128)(2,1)} %all-gather.15.cloned.1.call-done), kind=kOutput, calls=%fused_computation.245 | convolution fusion | flops 4294967296 | bytes 12582912 | tf_op jit(solution)/shard_map/gf,gd->fd/dot_general | solution.py:192
  530.4 38.3 %all-reduce.28 = (f32[1024]{0:T(1024)S(1)}, f32[1024]{0:T(1024)S(1)}, f32[1024]{0:T(1024)S(1)}, f32[1024]{0:T(1024)S(1)}, f32[1024]{0:T(1024)S(1)}, /*index=5*/f...) all-reduce(f32[1024]{0:T(1024)S(1)} %dynamic-update-slice.30, ...), channel_id=1, replica_groups=mesh['dp'=8,'tensor'=4] {'dp','tensor'}, use_global_device_ids=true, to_apply=%add.18 | all-reduce | flops 14336 | bytes 114688
  577.6 18.0 %reduce-scatter.22.cloned.1.call-done = f32[256,128]{1,0:T(8,128)} async-done(((f32[256,1024]{1,0:T(8,128)}), f32[256,128]{1,0:T(8,128)}) %reduce-scatter.22.cloned.1.call-update) | async-done | bytes 131088 | tf_op jit(solution)/shard_map/reduce_scatter | solution.py:194
  595.6 66.2 %reduce-scatter.20.cloned.1.call-done = f32[128,256]{1,0:T(8,128)} async-done(((f32[1024,256]{1,0:T(8,128)}), f32[128,256]{1,0:T(8,128)}) %reduce-scatter.20.cloned.1.call-update) | async-done | bytes 131088 | tf_op jit(solution)/shard_map/reduce_scatter | solution.py:271
  661.8 66.7 %reduce-scatter.18.cloned.1.call-done = f32[128,256]{1,0:T(8,128)} async-done(((f32[1024,256]{1,0:T(8,128)}), f32[128,256]{1,0:T(8,128)}) %reduce-scatter.18.cloned.1.call-update) | async-done | bytes 131088 | tf_op jit(solution)/shard_map/reduce_scatter | solution.py:270
  728.5 66.2 %reduce-scatter.16.cloned.1.call-done = f32[128,256]{1,0:T(8,128)} async-done(((f32[1024,256]{1,0:T(8,128)}), f32[128,256]{1,0:T(8,128)}) %reduce-scatter.16.cloned.1.call-update) | async-done | bytes 131088 | tf_op jit(solution)/shard_map/reduce_scatter | solution.py:269
  794.7 91.6 %reduce-scatter.24.cloned.1.call-done = f32[128,1024]{1,0:T(8,128)} async-done(((f32[1024,1024]{1,0:T(8,128)}), f32[128,1024]{1,0:T(8,128)}) %reduce-scatter.24.cloned.1.call-update) | async-done | bytes 524304 | tf_op jit(solution)/shard_map/reduce_scatter | solution.py:272
  886.3 92.3 %reduce-scatter.26.cloned.1.call-done = f32[1024,128]{1,0:T(8,128)} async-done(((f32[1024,1024]{1,0:T(8,128)}), f32[1024,128]{1,0:T(8,128)}) %reduce-scatter.26.cloned.1.call-update) | async-done | bytes 524304 | tf_op jit(solution)/shard_map/reduce_scatter | solution.py:195
  (425 shorter events, 194.6 us)
Async XLA Ops:
  7.2 229.4 %all-gather.7.cloned.1.call-start = ((), (), s32[]{:S(2)}) async-start(), calls=%async_computation.9 | async-start | bytes 5242880 | tf_op jit(solution)/shard_map/all_gather | solution.py:121
  8.7 56.8 %copy-start.97 = (f32[128]{0:T(128)S(1)}, f32[128]{0:T(128)}, u32[]{:S(2)}) copy-start(f32[128]{0:T(128)} %param.55) | copy-start | bytes 1540
  8.7 96.8 %copy-start.80 = (bf16[128,256]{1,0:T(8,128)(2,1)S(1)}, bf16[128,256]{1,0:T(8,128)(2,1)}, u32[]{:S(2)}) copy-start(bf16[128,256]{1,0:T(8,128)(2,1)} %param.46) | copy-start | bytes 196612
  8.7 130.2 %copy-start.72 = (f32[512]{0:T(512)}, f32[512]{0:T(512)S(1)}, u32[]{:S(2)}) copy-start(f32[512]{0:T(512)S(1)} %broadcast_multiply_fusion.1) | copy-start | bytes 6148
  8.7 130.2 %copy-start.81 = (bf16[128,256]{1,0:T(8,128)(2,1)S(1)}, bf16[128,256]{1,0:T(8,128)(2,1)}, u32[]{:S(2)}) copy-start(bf16[128,256]{1,0:T(8,128)(2,1)} %param.48) | copy-start | bytes 196612
  10.4 160.5 %copy-start.82 = (bf16[128,256]{1,0:T(8,128)(2,1)S(1)}, bf16[128,256]{1,0:T(8,128)(2,1)}, u32[]{:S(2)}) copy-start(bf16[128,256]{1,0:T(8,128)(2,1)} %param.50) | copy-start | bytes 196612
  58.8 80.2 %copy-start.76 = (f32[1024]{0:T(1024)}, f32[1024]{0:T(1024)S(1)}, u32[]{:S(2)}) copy-start(f32[1024]{0:T(1024)S(1)} %get-tuple-element.152) | copy-start | bytes 12292
  58.8 80.2 %copy-start.78 = (f32[1024]{0:T(1024)}, f32[1024]{0:T(1024)S(1)}, u32[]{:S(2)}) copy-start(f32[1024]{0:T(1024)S(1)} %get-tuple-element.154) | copy-start | bytes 12292
  58.8 144.2 %copy-start.83 = (bf16[256,128]{1,0:T(8,128)(2,1)S(1)}, bf16[256,128]{1,0:T(8,128)(2,1)}, u32[]{:S(2)}) copy-start(bf16[256,128]{1,0:T(8,128)(2,1)} %param.52) | copy-start | bytes 196612
  62.0 185.3 %all-gather.15.cloned.1.call-start = ((), (), s32[]{:S(2)}) async-start(), calls=%async_computation.14 | async-start | bytes 5242880 | tf_op jit(solution)/shard_map/all_gather | solution.py:190
  62.8 232.0 %all-gather.11.cloned.1.call-start = ((), (), s32[]{:S(2)}) async-start(), calls=%async_computation.11 | async-start | bytes 2359296 | tf_op jit(solution)/shard_map/all_gather | solution.py:132
  63.5 231.3 %all-gather.9.cloned.1.call-start = ((), (), s32[]{:S(2)}) async-start(), calls=%async_computation.10 | async-start | bytes 5242880 | tf_op jit(solution)/shard_map/all_gather | solution.py:122
  64.1 241.4 %all-gather.13.cloned.1.call-start = ((), (), s32[]{:S(2)}) async-start(), calls=%async_computation.12 | async-start | bytes 2359296 | tf_op jit(solution)/shard_map/all_gather | solution.py:182
  64.7 459.6 %reduce-scatter.14.cloned.1.call-start = ((), (), s32[]{:S(2)}) async-start(), calls=%async_computation.16 | async-start | bytes 5242880 | tf_op jit(solution)/shard_map/reduce_scatter | solution.py:292
  170.9 71.1 %copy-start.42 = (bf16[1024,256]{1,0:T(8,128)(2,1)}, bf16[1024,256]{1,0:T(8,128)(2,1)S(1)}, u32[]{:S(2)}) copy-start(bf16[1024,256]{1,0:T(8,128)(2,1)S(1)} %all_gather.70) | copy-start | bytes 1572868
  342.6 181.7 %reduce-scatter.12.cloned.1.call-start = ((), (), s32[]{:S(2)}) async-start(), calls=%async_computation.15 | async-start | bytes 5242880 | tf_op jit(solution)/shard_map/reduce_scatter | solution.py:289
  439.0 134.4 %reduce-scatter.10.cloned.1.call-start = ((), (), s32[]{:S(2)}) async-start(), calls=%async_computation.13 | async-start | bytes 5242880 | tf_op jit(solution)/shard_map/reduce_scatter | solution.py:186
  481.7 113.9 %reduce-scatter.22.cloned.1.call-start = ((), (), s32[]{:S(2)}) async-start(), calls=%async_computation.20 | async-start | bytes 1179648 | tf_op jit(solution)/shard_map/reduce_scatter | solution.py:194
  486.2 175.6 %reduce-scatter.20.cloned.1.call-start = ((), (), s32[]{:S(2)}) async-start(), calls=%async_computation.19 | async-start | bytes 1179648 | tf_op jit(solution)/shard_map/reduce_scatter | solution.py:271
  491.2 237.2 %reduce-scatter.18.cloned.1.call-start = ((), (), s32[]{:S(2)}) async-start(), calls=%async_computation.18 | async-start | bytes 1179648 | tf_op jit(solution)/shard_map/reduce_scatter | solution.py:270
  496.3 298.4 %reduce-scatter.16.cloned.1.call-start = ((), (), s32[]{:S(2)}) async-start(), calls=%async_computation.17 | async-start | bytes 1179648 | tf_op jit(solution)/shard_map/reduce_scatter | solution.py:269
  501.1 385.2 %reduce-scatter.24.cloned.1.call-start = ((), (), s32[]{:S(2)}) async-start(), calls=%async_computation.21 | async-start | bytes 4718592 | tf_op jit(solution)/shard_map/reduce_scatter | solution.py:272
  511.5 467.1 %reduce-scatter.26.cloned.1.call-start = ((), (), s32[]{:S(2)}) async-start(), calls=%async_computation.22 | async-start | bytes 4718592 | tf_op jit(solution)/shard_map/reduce_scatter | solution.py:195
  568.7 409.9 %copy-start.104 = (f32[32]{0:T(128)}, f32[32]{0:T(128)S(1)}, u32[]{:S(2)}) copy-start(f32[32]{0:T(128)S(1)} %dynamic-slice.66) | copy-start | bytes 388
  (112 other events, 831.2 us)
Sparse Core Ops, SparseCore 0:
  62.2 34.4 all-gather.6
  98.2 34.4 all-gather.14
  134.8 56.6 all-gather.10
  192.9 34.9 all-gather.8
  229.8 51.0 all-gather.12
  342.7 40.6 reduce-scatter.13
  439.1 41.1 reduce-scatter.11
  482.7 44.5 reduce-scatter.9
  531.7 63.8 reduce-scatter.21
  599.4 62.3 reduce-scatter.19
  666.2 62.2 reduce-scatter.17
  732.3 62.3 reduce-scatter.15
  799.3 86.9 reduce-scatter.23
  890.4 88.1 reduce-scatter.25
where the time goes:
time: 991 us; the launch traced here: 986 us
  waiting for transfers between devices  404 us (41%)
  blocking collectives  245 us (25%)
  matrix products  210 us (21%)
  other arithmetic  72.8 us (7%)
  local copies, waits for them, and re-layouts  37.6 us (4%)
  between operations  16 us (2%)
    reduce_scatter x1, waiting for transfers between devices, per_device(): lax.psum_scatter(grad_down, 'dp', scatter_dimension=1, tiled=True)  92.3 us
    reduce_scatter x1, waiting for transfers between devices, per_device(): lax.psum_scatter(grad_wu, 'dp', scatter_dimension=0, tiled=True)  91.6 us
    unnamed x2, blocking collectives  80.7 us
    reduce_scatter x1, waiting for transfers between devices, per_device(): lax.psum_scatter(grad_wk, 'dp', scatter_dimension=0, tiled=True)  66.7 us
    reduce_scatter x1, waiting for transfers between devices, per_device(): lax.psum_scatter(grad_wq, 'dp', scatter_dimension=0, tiled=True)  66.2 us
    reduce_scatter x1, waiting for transfers between devices, per_device(): lax.psum_scatter(grad_wv, 'dp', scatter_dimension=0, tiled=True)  66.2 us
    all_gather x1, blocking collectives, per_device(): lax.all_gather(b_up, ('dp', 'tensor'), axis=0, tiled=True)  40 us
    all_gather x1, blocking collectives, per_device(): lax.all_gather(w_query, 'dp', axis=0, tiled=True)  33.4 us
  transfers between devices with their start and end apart: 14, of which 6 were waited for; matrix products, arithmetic and copies ran while one was open for 25% of the time, Pallas kernels for 0%

commit v1 on v0

--- a/solution.py
+++ b/solution.py
@@ -1,8 +1,11 @@
+import functools
 import math
 
 import jax
 import jax.numpy as jnp
 from jax import lax
+from jax.experimental import pallas as pl
+from jax.experimental.pallas import tpu as pltpu
 from jax.sharding import PartitionSpec as P
 
 HEAD = 64
@@ -60,7 +63,370 @@
     return jnp.concatenate([turned_part, head_vals[..., rot_dims:]], -1)
 
 
+RING = 8
+VMEM_BYTES = 56 * 1024 * 1024
+MESH_ID = pl.DeviceIdType.MESH
+STREAMS = ((0, 0, 64, 1), (1, 0, 640, -1), (0, 64, 48, 1), (1, 640, 640, -1), (0, 112, 16, -1))
+
+
+def ring_to_dp(place):
+    place = (place + 2 * RING) % RING
+    upper = place // (RING // 2)
+    return 2 * place + upper * (2 * RING - 1 - 4 * place)
+
+
+def partners():
+    dp_at = lax.axis_index("dp")
+    tensor_at = lax.axis_index("tensor")
+    depth, side = dp_at // 2, dp_at % 2
+    place = depth + side * (RING - 1 - 2 * depth)
+    sibling = tensor_at + 1 - 2 * (tensor_at % 2)
+    across = (tensor_at + 2) % 4
+    return (dp_at, tensor_at, place, sibling, across)
+
+
+def meet(devices):
+    barrier = pltpu.get_barrier_semaphore()
+    for device in devices:
+        pl.semaphore_signal(barrier, inc=1, device_id=device, device_id_type=MESH_ID)
+    pl.semaphore_wait(barrier, len(devices))
+
+
+def remote(source, target, send, recv, device):
+    return pltpu.make_async_remote_copy(
+        src_ref=source,
+        dst_ref=target,
+        send_sem=send,
+        recv_sem=recv,
+        device_id=device,
+        device_id_type=MESH_ID,
+    )
+
+
+def gather_kernel(
+    tok, cot, small, w_in, w_out, tok_all, cot_all, small_all, in_all, out_all,
+    local_sem, tsend, trecv, fsend, frecv, rsend, rrecv, ssend, srecv,
+):
+    dp_at, tensor_at, place, sibling, across = partners()
+    right = (ring_to_dp(place + 1), tensor_at)
+    left = (ring_to_dp(place - 1), tensor_at)
+    sib = (dp_at, sibling)
+    opp = (dp_at, across)
+    meet((right, left, sib, opp))
+    blocks = (w_in, w_out)
+    fulls = (in_all, out_all)
+    sends = []
+
+    def ring_copy(number, step, owner):
+        which, low, rows, way = STREAMS[number]
+        here = fulls[which].at[owner, pl.ds(low, rows)]
+        source = blocks[which].at[pl.ds(low, rows)] if step == 0 else here
+        return remote(
+            source, here, rsend.at[number, step], rrecv.at[number, step], right if way > 0 else left
+        )
+
+    def small_ring(step, owner):
+        return remote(
+            small_all.at[owner], small_all.at[owner], ssend.at[step], srecv.at[step], right
+        )
+
+    for number in range(len(STREAMS)):
+        copy = ring_copy(number, 0, dp_at)
+        copy.start()
+        sends.append(copy)
+    mine = ((small, small_all.at[dp_at]), (tok, tok_all), (cot, cot_all))
+    for number, (own, full) in enumerate(mine):
+        for peer, device in enumerate((opp, sib)):
+            copy = remote(
+                own, full.at[tensor_at], tsend.at[number, peer], trecv.at[number, peer], device
+            )
+            copy.start()
+            sends.append(copy)
+    locals_ = [
+        pltpu.make_async_copy(own, full.at[tensor_at], local_sem.at[number])
+        for number, (own, full) in enumerate(mine)
+    ]
+    locals_.append(pltpu.make_async_copy(w_in, in_all.at[dp_at], local_sem.at[3]))
+    locals_.append(pltpu.make_async_copy(w_out, out_all.at[dp_at], local_sem.at[4]))
+    for copy in locals_:
+        copy.start()
+
+    def forward(number):
+        full = mine[number][1]
+        remote(
+            full.at[across], full.at[across], tsend.at[number, 0], trecv.at[number, 0], opp
+        ).wait_recv()
+        copy = remote(full.at[across], full.at[across], fsend.at[number], frecv.at[number], sib)
+        copy.start()
+        sends.append(copy)
+
+    def settle(number):
+        full = mine[number][1]
+        remote(
+            full.at[sibling], full.at[sibling], tsend.at[number, 1], trecv.at[number, 1], sib
+        ).wait_recv()
+        last = (sibling + 2) % 4
+        remote(
+            full.at[last], full.at[last], fsend.at[number], frecv.at[number], sib
+        ).wait_recv()
+
+    for copy in locals_:
+        copy.wait()
+    forward(0)
+    settle(0)
+    copy = small_ring(0, dp_at)
+    copy.start()
+    sends.append(copy)
+    for step in range(1, RING):
+        for number, (_, _, _, way) in enumerate(STREAMS):
+            owner = ring_to_dp(place - way * step)
+            arrived = fulls[STREAMS[number][0]].at[owner, pl.ds(STREAMS[number][1], STREAMS[number][2])]
+            remote(
+                arrived, arrived, rsend.at[number, step - 1], rrecv.at[number, step - 1], right
+            ).wait_recv()
+            if step < RING - 1:
+                copy = ring_copy(number, step, owner)
+                copy.start()
+                sends.append(copy)
+        owner = ring_to_dp(place - step)
+        small_ring(step - 1, owner).wait_recv()
+        if step < RING - 1:
+            copy = small_ring(step, owner)
+            copy.start()
+            sends.append(copy)
+        if step == 4:
+            forward(1)
+    forward(2)
+    settle(1)
+    settle(2)
+    for copy in sends:
+        copy.wait_send()
+
+
+def gather_all(tok, cot, small, w_in, w_out):
+    anywhere = pl.BlockSpec(memory_space=pl.ANY)
+    shape = jax.ShapeDtypeStruct
+    dma = pltpu.SemaphoreType.DMA
+    return pl.pallas_call(
+        gather_kernel,
+        out_shape=(
+            shape((4,) + tok.shape, tok.dtype),
+            shape((4,) + cot.shape, cot.dtype),
+            shape((RING, 4) + small.shape, small.dtype),
+            shape((RING,) + w_in.shape, w_in.dtype),
+            shape((RING,) + w_out.shape, w_out.dtype),
+        ),
+        in_specs=[anywhere] * 5,
+        out_specs=(anywhere,) * 5,
+        scratch_shapes=[
+            dma((5,)),
+            dma((3, 2)),
+            dma((3, 2)),
+            dma((3,)),
+            dma((3,)),
+            dma((len(STREAMS), RING - 1)),
+            dma((len(STREAMS), RING - 1)),
+            dma((RING - 1,)),
+            dma((RING - 1,)),
+        ],
+        compiler_params=pltpu.CompilerParams(collective_id=0, has_side_effects=True),
+    )(tok, cot, small, w_in, w_out)
+
+
+def add_rows(target, terms, step):
+    rows = target.shape[0]
+
+    @pl.loop(0, rows // step)
+    def _(at):
+        here = pl.ds(pl.multiple_of(at * step, step), step)
+        total = terms[0][here].astype(jnp.float32)
+        for term in terms[1:]:
+            total = total + term[here].astype(jnp.float32)
+        target[here] = total.astype(target.dtype)
+
+
+def scatter_kernel(
+    parts, g_in, g_out, shares, own_in, own_out,
+    slot_in, slot_out, core_buf, cross_buf, rsend, rrecv, csend, crecv, xsend, xrecv,
+):
+    dp_at, tensor_at, place, sibling, across = partners()
+    right = (ring_to_dp(place + 1), tensor_at)
+    left = (ring_to_dp(place - 1), tensor_at)
+    sib = (dp_at, sibling)
+    opp = (dp_at, across)
+    meet((right, left, sib, opp))
+    grads = (g_in, g_out)
+    slots = (slot_in, slot_out)
+    owns = (own_in, own_out)
+    sends = []
+
+    def slot_of(number, step):
+        which, low, rows, _ = STREAMS[number]
+        return slots[which].at[step, pl.ds(low, rows)]
+
+    def grad_of(number, owner):
+        which, low, rows, _ = STREAMS[number]
+        return grads[which].at[owner, pl.ds(low, rows)]
+
+    def ring_copy(number, step, source):
+        way = STREAMS[number][3]
+        return remote(
+            source,
+            slot_of(number, step),
+            rsend.at[number, step],
+            rrecv.at[number, step],
+            right if way > 0 else left,
+        )
+
+    for number, (_, _, _, way) in enumerate(STREAMS):
+        copy = ring_copy(number, 0, grad_of(number, ring_to_dp(place - way)))
+        copy.start()
+        sends.append(copy)
+    count = parts.shape[0]
+    across_sib = (sibling + 2) % 4
+    for number in range(count):
+        copy = remote(
+            parts.at[number, across_sib],
+            core_buf.at[number, 0],
+            csend.at[number, 0],
+            crecv.at[number, 0],
+            sib,
+        )
+        copy.start()
+        sends.append(copy)
+    for number in range(count):
+        copy = remote(
+            parts.at[number, sibling],
+            core_buf.at[number, 1],
+            csend.at[number, 1],
+            crecv.at[number, 1],
+            sib,
+        )
+        copy.start()
+        sends.append(copy)
+
+    def cross(number):
+        buf = core_buf.at[number, 0]
+        remote(buf, buf, csend.at[number, 0], crecv.at[number, 0], sib).wait_recv()
+        add_rows(buf, (buf, parts.at[number, across]), 64)
+        copy = remote(buf, cross_buf.at[number], xsend.at[number], xrecv.at[number], opp)
+        copy.start()
+        sends.append(copy)
+
+    for number in range(count):
+        cross(number)
+    for step in range(RING - 1):
+        for number, (which, low, rows, way) in enumerate(STREAMS):
+            here = slot_of(number, step)
+            remote(
+                here, here, rsend.at[number, step], rrecv.at[number, step], right
+            ).wait_recv()
+            term = grad_of(number, ring_to_dp(place - way * (2 + step)))
+            if step < RING - 2:
+                add_rows(here, (here, term), 80 if which else 16)
+                copy = ring_copy(number, step + 1, here)
+                copy.start()
+                sends.append(copy)
+            else:
+                add_rows(owns[which].at[pl.ds(low, rows)], (here, term), 80 if which else 16)
+    for number in range(count):
+        buf = core_buf.at[number, 1]
+        remote(buf, buf, csend.at[number, 1], crecv.at[number, 1], sib).wait_recv()
+        other = cross_buf.at[number]
+        remote(other, other, xsend.at[number], xrecv.at[number], opp).wait_recv()
+        add_rows(shares.at[number], (buf, other, parts.at[number, tensor_at]), 64)
+    for copy in sends:
+        copy.wait_send()
+
+
+def scatter_all(parts, g_in, g_out):
+    inside = pl.BlockSpec(memory_space=pltpu.VMEM)
+    shape = jax.ShapeDtypeStruct
+    dma = pltpu.SemaphoreType.DMA
+    count, _, rows, width = parts.shape
+    return pl.pallas_call(
+        scatter_kernel,
+        out_shape=(
+            shape((count, rows, width), jnp.bfloat16),
+            shape(g_in.shape[1:], jnp.float32),
+            shape(g_out.shape[1:], jnp.float32),
+        ),
+        in_specs=[inside] * 3,
+        out_specs=(inside,) * 3,
+        scratch_shapes=[
+            pltpu.VMEM((RING - 1,) + g_in.shape[1:], jnp.bfloat16),
+            pltpu.VMEM((RING - 1,) + g_out.shape[1:], jnp.bfloat16),
+            pltpu.VMEM((count, 2, rows, width), jnp.bfloat16),
+            pltpu.VMEM((count, rows, width), jnp.bfloat16),
+            dma((len(STREAMS), RING - 1)),
+            dma((len(STREAMS), RING - 1)),
+            dma((count, 2)),
+            dma((count, 2)),
+            dma((count,)),
+            dma((count,)),
+        ],
+        compiler_params=pltpu.CompilerParams(
+            collective_id=1, has_side_effects=True, vmem_limit_bytes=VMEM_BYTES
+        ),
+    )(parts, g_in, g_out)
+
+
+def sum_kernel(terms, total, first, middle, second, asend, arecv, bsend, brecv):
+    dp_at = lax.axis_index("dp")
+    tensor_at = lax.axis_index("tensor")
+    peers = [(dp_at, (tensor_at + gap) % 4) for gap in range(1, 4)]
+    rows = [((dp_at + gap) % RING, tensor_at) for gap in range(1, RING)]
+    meet(peers + rows)
+    sends = []
+    for gap, device in enumerate(peers):
+        copy = remote(
+            terms.at[device[1]], first.at[gap], asend.at[gap], arecv.at[gap], device
+        )
+        copy.start()
+        sends.append(copy)
+    for copy in sends:
+        copy.wait_recv()
+    middle[...] = terms[tensor_at] + first[0] + first[1] + first[2]
+    seconds = []
+    for gap, device in enumerate(rows):
+        copy = remote(
+            middle.at[device[0]], second.at[gap], bsend.at[gap], brecv.at[gap], device
+        )
+        copy.start()
+        seconds.append(copy)
+    for copy in seconds:
+        copy.wait_recv()
+    result = middle[dp_at]
+    for gap in range(RING - 1):
+        result = result + second[gap]
+    total[...] = result
+    for copy in sends + seconds:
+        copy.wait_send()
+
+
+def sum_all(terms):
+    inside = pl.BlockSpec(memory_space=pltpu.VMEM)
+    dma = pltpu.SemaphoreType.DMA
+    return pl.pallas_call(
+        sum_kernel,
+        out_shape=jax.ShapeDtypeStruct(terms.shape[2:], jnp.float32),
+        in_specs=[inside],
+        out_specs=inside,
+        scratch_shapes=[
+            pltpu.VMEM((3,) + terms.shape[1:], jnp.float32),
+            pltpu.VMEM(terms.shape[1:], jnp.float32),
+            pltpu.VMEM((RING - 1,) + terms.shape[2:], jnp.float32),
+            dma((3,)),
+            dma((3,)),
+            dma((RING - 1,)),
+            dma((RING - 1,)),
+        ],
+        compiler_params=pltpu.CompilerParams(collective_id=2, has_side_effects=True),
+    )(terms)
+
+
 def per_device(
+    ring,
     tokens,
     out_grad,
     seq_lengths,
@@ -81,18 +447,36 @@
     w_down,
     b_down,
 ):
-    gathered_small = (
-        lax.all_gather(norm1_gain, ("dp", "tensor"), axis=0, tiled=True),
-        lax.all_gather(norm1_bias, ("dp", "tensor"), axis=0, tiled=True),
-        lax.all_gather(norm2_gain, ("dp", "tensor"), axis=0, tiled=True),
-        lax.all_gather(norm2_bias, ("dp", "tensor"), axis=0, tiled=True),
-        lax.all_gather(b_query, ("dp", "tensor"), axis=0, tiled=True),
-        lax.all_gather(b_key, ("dp", "tensor"), axis=0, tiled=True),
-        lax.all_gather(b_value, ("dp", "tensor"), axis=0, tiled=True),
-        lax.all_gather(b_dense, ("dp", "tensor"), axis=0, tiled=True),
-        lax.all_gather(b_up, ("dp", "tensor"), axis=0, tiled=True),
-        lax.all_gather(b_down, ("dp", "tensor"), axis=0, tiled=True),
-    )
+    vectors = (
+        norm1_gain, norm1_bias, norm2_gain, norm2_bias,
+        b_query, b_key, b_value, b_dense, b_down, b_up,
+    )
+    sizes = [vector.shape[0] for vector in vectors]
+    packed = jnp.concatenate(vectors)
+    w_in = jnp.concatenate([w_query, w_key, w_value, w_up], 1)
+    w_out = jnp.concatenate([w_dense, w_down], 0)
+    if ring:
+        packed = jnp.pad(packed, (0, 1024 - packed.shape[0])).reshape(8, 128)
+        tok_all, grad_group, packed_all, w_in, w_out = gather_all(
+            tokens, out_grad, packed, w_in, w_out
+        )
+        tok_all = tok_all.reshape(-1, tokens.shape[1])
+        grad_group = grad_group.reshape(-1, tokens.shape[1])
+        packed_all = packed_all.reshape(4 * RING, 1024)
+        w_in = w_in.reshape(-1, w_in.shape[2])
+        w_out = w_out.transpose(1, 0, 2).reshape(w_out.shape[1], -1)
+    else:
+        packed_all = lax.all_gather(packed, ("dp", "tensor"), axis=0)
+        packed_all = packed_all.reshape(-1, packed.shape[0])
+        tok_all = lax.all_gather(tokens, "tensor", axis=0, tiled=True)
+        grad_group = lax.all_gather(out_grad, "tensor", axis=0, tiled=True)
+        w_in = lax.all_gather(w_in, "dp", axis=0, tiled=True)
+        w_out = lax.all_gather(w_out, "dp", axis=1, tiled=True)
+    gathered_small = []
+    start = 0
+    for size in sizes:
+        gathered_small.append(packed_all[:, start : start + size].reshape(-1))
+        start += size
     (
         gain_one,
         shift_one,
@@ -102,8 +486,8 @@
         bias_key,
         bias_value,
         bias_dense,
+        bias_down,
         bias_up,
-        bias_down,
     ) = gathered_small
     width = tokens.shape[1]
     column_count = w_query.shape[1]
@@ -115,26 +499,20 @@
     bias_value = lax.dynamic_slice_in_dim(bias_value, tensor_at * column_count, column_count)
     bias_up = lax.dynamic_slice_in_dim(bias_up, tensor_at * hidden_count, hidden_count)
     own_rows = tokens.astype(jnp.float32)
-    normed_one = layer_norm(own_rows, gain_one, shift_one).astype(jnp.bfloat16)
-    normed_two = layer_norm(own_rows, gain_two, shift_two).astype(jnp.bfloat16)
-    normed_one, normed_two = (
-        lax.all_gather(normed_one, "tensor", axis=0, tiled=True),
-        lax.all_gather(normed_two, "tensor", axis=0, tiled=True),
-    )
+    all_rows = tok_all.astype(jnp.float32)
+    normed_one = layer_norm(all_rows, gain_one, shift_one).astype(jnp.bfloat16)
+    normed_two = layer_norm(all_rows, gain_two, shift_two).astype(jnp.bfloat16)
     group_size = normed_one.shape[0]
     row_index, segment, positions = segment_rows(seq_lengths.reshape(-1), group_size)
     cosine_table, sine_table = rotary_tables(positions, ROTARY)
     score_scale = 1.0 / math.sqrt(HEAD)
-    pieces = (
-        lax.all_gather(w_query, "dp", axis=0, tiled=True),
-        lax.all_gather(w_key, "dp", axis=0, tiled=True),
-        lax.all_gather(w_value, "dp", axis=0, tiled=True),
-        lax.all_gather(w_up, "dp", axis=0, tiled=True),
-    )
-    query_raw = jnp.dot(normed_one, pieces[0], preferred_element_type=jnp.float32)
-    key_raw = jnp.dot(normed_one, pieces[1], preferred_element_type=jnp.float32)
-    value_raw = jnp.dot(normed_one, pieces[2], preferred_element_type=jnp.float32)
-    up_raw = jnp.dot(normed_two, pieces[3], preferred_element_type=jnp.float32)
+    w_qkv = w_in[:, : 3 * column_count]
+    w_hidden = w_in[:, 3 * column_count :]
+    qkv_raw = jnp.dot(normed_one, w_qkv, preferred_element_type=jnp.float32)
+    query_raw = qkv_raw[:, :column_count]
+    key_raw = qkv_raw[:, column_count : 2 * column_count]
+    value_raw = qkv_raw[:, 2 * column_count :]
+    up_raw = jnp.dot(normed_two, w_hidden, preferred_element_type=jnp.float32)
     queries = rotate(
         (query_raw + bias_query).reshape(group_size, heads_here, HEAD), cosine_table, sine_table
     ).astype(jnp.bfloat16)
@@ -177,31 +555,15 @@
     )
     hidden_pre = up_raw + bias_up
     activated = smooth(hidden_pre).astype(jnp.bfloat16)
-    pieces = (
-        lax.all_gather(w_dense, "dp", axis=1, tiled=True),
-        lax.all_gather(w_down, "dp", axis=1, tiled=True),
-    )
-    partial_cols = jnp.dot(context, pieces[0], preferred_element_type=jnp.float32)
-    partial_cols = partial_cols + jnp.dot(activated, pieces[1], preferred_element_type=jnp.float32)
-    summed = lax.psum_scatter(
-        partial_cols.astype(jnp.bfloat16), "tensor", scatter_dimension=0, tiled=True
-    ).astype(jnp.float32)
-    layer_out = (own_rows + summed + bias_dense + bias_down).astype(jnp.bfloat16)
-    grad_group = lax.all_gather(out_grad, "tensor", axis=0, tiled=True)
-    grad_dense = jnp.einsum("gc,gd->cd", context, grad_group, preferred_element_type=jnp.float32)
-    grad_down = jnp.einsum("gf,gd->fd", activated, grad_group, preferred_element_type=jnp.float32)
-    grad_dense, grad_down = (
-        lax.psum_scatter(grad_dense, "dp", scatter_dimension=1, tiled=True),
-        lax.psum_scatter(grad_down, "dp", scatter_dimension=1, tiled=True),
-    )
-    pieces = (
-        lax.all_gather(w_dense, "dp", axis=1, tiled=True),
-        lax.all_gather(w_down, "dp", axis=1, tiled=True),
-    )
+    joined = jnp.concatenate([context, activated], 1)
+    partial_cols = jnp.dot(joined, w_out, preferred_element_type=jnp.float32).astype(jnp.bfloat16)
+    grad_out = jnp.einsum("gf,gd->fd", joined, grad_group, preferred_element_type=jnp.float32)
     grad_context = jnp.einsum(
-        "gd,cd->gc", grad_group, pieces[0], preferred_element_type=jnp.float32
-    )
-    grad_act = jnp.einsum("gd,fd->gf", grad_group, pieces[1], preferred_element_type=jnp.float32)
+        "gd,cd->gc", grad_group, w_out[:column_count], preferred_element_type=jnp.float32
+    )
+    grad_act = jnp.einsum(
+        "gd,fd->gf", grad_group, w_out[column_count:], preferred_element_type=jnp.float32
+    )
     grad_context = grad_context.astype(jnp.bfloat16).reshape(group_size, heads_here, HEAD)
     gelu_value, gelu_back = jax.vjp(smooth, hidden_pre)
     grad_hidden = gelu_back(grad_act)[0].astype(jnp.bfloat16)
@@ -261,38 +623,45 @@
     )
     grad_key = rotate_back(key_total)[0].reshape(group_size, column_count).astype(jnp.bfloat16)
     grad_value = value_total.reshape(group_size, column_count).astype(jnp.bfloat16)
-    grad_wq = jnp.einsum("gd,gc->dc", normed_one, grad_query, preferred_element_type=jnp.float32)
-    grad_wk = jnp.einsum("gd,gc->dc", normed_one, grad_key, preferred_element_type=jnp.float32)
-    grad_wv = jnp.einsum("gd,gc->dc", normed_one, grad_value, preferred_element_type=jnp.float32)
+    grad_qkv = jnp.concatenate([grad_query, grad_key, grad_value], 1)
+    grad_wqkv = jnp.einsum("gd,gc->dc", normed_one, grad_qkv, preferred_element_type=jnp.float32)
     grad_wu = jnp.einsum("gd,gf->df", normed_two, grad_hidden, preferred_element_type=jnp.float32)
+    part_one = jnp.einsum(
+        "gc,dc->gd", grad_qkv, w_qkv, preferred_element_type=jnp.float32
+    ).astype(jnp.bfloat16)
+    part_two = jnp.einsum(
+        "gf,df->gd", grad_hidden, w_hidden, preferred_element_type=jnp.float32
+    ).astype(jnp.bfloat16)
+    grad_in = jnp.concatenate(
+        [grad_wqkv.astype(jnp.bfloat16), grad_wu.astype(jnp.bfloat16)], 1
+    )
+    grad_out = grad_out.astype(jnp.bfloat16)
+    if ring:
+        own_count = tokens.shape[0]
+        parts = jnp.stack([partial_cols, part_one, part_two]).reshape(3, 4, own_count, width)
+        shares, grad_in, grad_out = scatter_all(
+            parts,
+            grad_in.reshape(RING, width // RING, -1),
+            grad_out.reshape(-1, RING, width // RING).transpose(1, 0, 2),
+        )
+        summed, share_one, share_two = (shares[number].astype(jnp.float32) for number in range(3))
+    else:
+        summed, share_one, share_two = (
+            lax.psum_scatter(part, "tensor", scatter_dimension=0, tiled=True).astype(jnp.float32)
+            for part in (partial_cols, part_one, part_two)
+        )
+        grad_in = lax.psum_scatter(grad_in, "dp", scatter_dimension=0, tiled=True)
+        grad_out = lax.psum_scatter(grad_out, "dp", scatter_dimension=1, tiled=True)
+    grad_in = grad_in.astype(jnp.float32)
+    grad_out = grad_out.astype(jnp.float32)
     grads_in = (
-        lax.psum_scatter(grad_wq, "dp", scatter_dimension=0, tiled=True),
-        lax.psum_scatter(grad_wk, "dp", scatter_dimension=0, tiled=True),
-        lax.psum_scatter(grad_wv, "dp", scatter_dimension=0, tiled=True),
-        lax.psum_scatter(grad_wu, "dp", scatter_dimension=0, tiled=True),
-    )
-    pieces = (
-        lax.all_gather(w_query, "dp", axis=0, tiled=True),
-        lax.all_gather(w_key, "dp", axis=0, tiled=True),
-        lax.all_gather(w_value, "dp", axis=0, tiled=True),
-        lax.all_gather(w_up, "dp", axis=0, tiled=True),
-    )
-    part_one = jnp.einsum("gc,dc->gd", grad_query, pieces[0], preferred_element_type=jnp.float32)
-    part_one = part_one + jnp.einsum(
-        "gc,dc->gd", grad_key, pieces[1], preferred_element_type=jnp.float32
-    )
-    part_one = part_one + jnp.einsum(
-        "gc,dc->gd", grad_value, pieces[2], preferred_element_type=jnp.float32
-    )
-    part_two = jnp.einsum("gf,df->gd", grad_hidden, pieces[3], preferred_element_type=jnp.float32)
-    share_one, share_two = (
-        lax.psum_scatter(
-            part_one.astype(jnp.bfloat16), "tensor", scatter_dimension=0, tiled=True
-        ).astype(jnp.float32),
-        lax.psum_scatter(
-            part_two.astype(jnp.bfloat16), "tensor", scatter_dimension=0, tiled=True
-        ).astype(jnp.float32),
-    )
+        grad_in[:, :column_count],
+        grad_in[:, column_count : 2 * column_count],
+        grad_in[:, 2 * column_count : 3 * column_count],
+        grad_in[:, 3 * column_count :],
+    )
+    grad_dense, grad_down = grad_out[:column_count], grad_out[column_count:]
+    layer_out = (own_rows + summed + bias_dense + bias_down).astype(jnp.bfloat16)
     normed_val_one, back_one = jax.vjp(layer_norm, own_rows, gain_one, shift_one)
     normed_val_two, back_two = jax.vjp(layer_norm, own_rows, gain_two, shift_two)
     input_one, d_gain_one, d_shift_one = back_one(share_one)
@@ -305,37 +674,35 @@
         )
 
     bias_sum = jnp.sum(out_grad, axis=0, dtype=jnp.float32)
-    small_grads = (
-        lax.psum_scatter(d_gain_one, ("dp", "tensor"), scatter_dimension=0, tiled=True),
-        lax.psum_scatter(d_shift_one, ("dp", "tensor"), scatter_dimension=0, tiled=True),
-        lax.psum_scatter(d_gain_two, ("dp", "tensor"), scatter_dimension=0, tiled=True),
-        lax.psum_scatter(d_shift_two, ("dp", "tensor"), scatter_dimension=0, tiled=True),
-        lax.psum_scatter(
-            placed(jnp.sum(grad_query, axis=0, dtype=jnp.float32), width),
-            ("dp", "tensor"),
-            scatter_dimension=0,
-            tiled=True,
-        ),
-        lax.psum_scatter(
-            placed(jnp.sum(grad_key, axis=0, dtype=jnp.float32), width),
-            ("dp", "tensor"),
-            scatter_dimension=0,
-            tiled=True,
-        ),
-        lax.psum_scatter(
-            placed(jnp.sum(grad_value, axis=0, dtype=jnp.float32), width),
-            ("dp", "tensor"),
-            scatter_dimension=0,
-            tiled=True,
-        ),
-        lax.psum_scatter(bias_sum, ("dp", "tensor"), scatter_dimension=0, tiled=True),
-        lax.psum_scatter(
-            placed(jnp.sum(grad_hidden, axis=0, dtype=jnp.float32), FF),
-            ("dp", "tensor"),
-            scatter_dimension=0,
-            tiled=True,
-        ),
-    )
+    devices = packed_all.shape[0]
+    small_terms = jnp.concatenate(
+        [
+            vector.reshape(devices, -1)
+            for vector in (
+                d_gain_one,
+                d_shift_one,
+                d_gain_two,
+                d_shift_two,
+                placed(jnp.sum(grad_query, axis=0, dtype=jnp.float32), width),
+                placed(jnp.sum(grad_key, axis=0, dtype=jnp.float32), width),
+                placed(jnp.sum(grad_value, axis=0, dtype=jnp.float32), width),
+                bias_sum,
+                placed(jnp.sum(grad_hidden, axis=0, dtype=jnp.float32), FF),
+            )
+        ],
+        1,
+    )
+    if ring:
+        small_terms = jnp.pad(small_terms, ((0, 0), (0, 1024 - small_terms.shape[1])))
+        small_terms = small_terms.reshape(RING, 4, 8, 128).transpose(1, 0, 2, 3)
+        small_total = sum_all(small_terms).reshape(-1)
+    else:
+        small_total = lax.psum_scatter(
+            small_terms, ("dp", "tensor"), scatter_dimension=0, tiled=True
+        ).reshape(-1)
+    each = width // devices
+    small_grads = [small_total[at * each : (at + 1) * each] for at in range(8)]
+    small_grads.append(small_total[8 * each : 8 * each + FF // devices])
     return (
         layer_out,
         tokens_grad,
@@ -400,6 +767,7 @@
         P("tensor", "dp"),
         P(("dp", "tensor")),
     )
+    ring = mesh.shape["dp"] == RING and mesh.shape["tensor"] == 4
     return jax.shard_map(
-        per_device, mesh=mesh, in_specs=in_specs, out_specs=out_specs, check_vma=False
-    )
+        functools.partial(per_device, ring), mesh=mesh, in_specs=in_specs, out_specs=out_specs, check_vma=False
+    )

time: 991 us -> 579 us (0.58)
  waiting for transfers between devices: 404 us -> 0 us
  Pallas kernels: 0 us -> 248 us
  blocking collectives: 245 us -> 0 us
  matrix products: 210 us -> 171 us
  other arithmetic: 72.8 us -> 99.7 us
  between operations: 16 us -> 2.16 us
  local copies, waits for them, and re-layouts: 37.6 us -> 49.9 us
    reduce_scatter x9 -> x0, waiting for transfers between devices: 401 us -> none  [the longest x1 92.3 us: per_device(): lax.psum_scatter(grad_down, 'dp', scatter_dimension=1, tiled=True)]
    pallas_call x0 -> x3, Pallas kernels: none -> 248 us  [the longest x1 153 us: gather_all(): pl.pallas_call(gather_kernel, out_shape=(shape((4,) + tok.shape, tok.dtyp...]
    all_gather x5 -> x0, blocking collectives: 165 us -> none  [the longest x1 40 us: per_device(): lax.all_gather(b_up, ('dp', 'tensor'), axis=0, tiled=True)]
    unnamed x2 -> x0, blocking collectives: 80.7 us -> none
    dot_general x17 -> x9, matrix products: 113 us -> 77.4 us  [the longest x1 25.6 us: per_device(): jnp.einsum('gd,fd->gf', grad_group, w_out[column_count:], preferred_eleme...]
    unnamed x271 -> x120, local copies, waits for them, and re-layouts: 31.7 us -> 8.01 us
    slice x1 -> x11, local copies, waits for them, and re-layouts: 0.01 us -> 16.4 us  [the longest x2 5.35 us: per_device(): w_out[column_count:]]
    reduce_sum x4, other arithmetic: 13.1 us -> 23.7 us  [per_device(): row_total = jnp.sum(expd, axis=-1, keepdims=True)]
  transfers between devices with their start and end apart: 14 -> 0, of which waited for: 6 -> 0; matrix products, arithmetic and copies ran while one was open for 25% -> 0% of each run, Pallas kernels for 0% -> 0%
where the time goes in v1:
time: 579 us; the launch traced here: 571 us
  Pallas kernels  248 us (43%)
  matrix products  171 us (30%)
  other arithmetic  99.7 us (17%)
  local copies, waits for them, and re-layouts  49.9 us (9%)
    pallas_call x1, Pallas kernels, gather_all(): pl.pallas_call(gather_kernel, out_shape=(shape((4,) + tok.shape, tok.dtyp...  153 us
    pallas_call x1, Pallas kernels, scatter_all(): pl.pallas_call(scatter_kernel, out_shape=(shape((count, rows, width), jnp...  84.5 us
    dot_general x1, matrix products, per_device(): jnp.einsum('gd,fd->gf', grad_group, w_out[column_count:], preferred_eleme...  25.6 us
    dot_general x4, matrix products, per_device(): jnp.einsum('qhd,khd->hqk', grad_blk, values[:high_row], preferred_element...  24.8 us
    reduce_sum x4, other arithmetic, per_device(): row_total = jnp.sum(expd, axis=-1, keepdims=True)  23.7 us
    convert_element_type x4, other arithmetic, per_device(): grad_scores = (probs_full * (grad_probs - row_inner)).astype(jnp.bfloat16)  20 us
    dot_general x4, matrix products, per_device(): jnp.einsum('hqk,qhd->khd', probs_full.astype(jnp.bfloat16), grad_blk, pre...  16.2 us
    dot_general x4, matrix products, per_device(): jnp.einsum('hqk,khd->qhd', attn_probs, values[:high_row], preferred_eleme...  16 us

profile of v1, /device:TPU:0, one launch (start us, length us, event | category | flops | bytes accessed | tf_op | source)
XLA Modules:
  0.0 570.9 jit_solution(10065989318979498860)
XLA Ops:
  16.4 153.0 %shard_map.332 = (bf16[4,512,1024]{2,1,0:T(8,128)(2,1)}, bf16[4,512,1024]{2,1,0:T(8,128)(2,1)}, f32[8,4,8,128]{3,2,1,0:T(8,128)}, bf16[8,128,1792]{2,1,0:T(8,128)(2,1)}, bf16[8,1280,128]{2,1,0:T(8,128)(2,1)}) custom-call(bf16[512,1024]{1,0:T(8,128)(2,1)} %tok.1, bf16[512,1024]{1,0:T(8,128)(2,1)} %cot.1, f32[8,128]{1,0:T(8,128)} %pad_bitcast_fusion.1.small, ...), custom_call_target="tpu_custom_call" | custom-call | tf_op jit(solution)/shard_map/pallas_call | solution.py:210
  190.8 5.5 add_convert_fusion.2
  216.6 13.1 %fusion.15 = f32[4,512]{1,0:T(4,128)S(1)} fusion(f32[4,512,1024]{2,1,0:T(8,128)S(1)} %get-tuple-element.223, f32[4,512]{1,0:T(4,128)S(1)} %get-tuple-element.222), kind=kLoop, calls=%fused_computation.49 | loop fusion | flops 4192256 | bytes 8404992 | tf_op jit(solution)/shard_map/reduce_sum | solution.py:545
  247.7 25.6 %convert_reduce_fusion = (f32[1024]{0:T(1024)S(1)}, bf16[2048,1024]{1,0:T(8,128)(2,1)S(1)}, f32[2048,1024]{1,0:T(8,128)}) fusion(f32[2048,1024]{1,0:T(8,128)S(1)} %fusion.78, f32[1024]{0:T(1024)S(1)} %dynamic_slice.15, bf16[2048,1024]{1,0:T(8,128)(2,1)S(1)} %bitcast.262, bf16[1024,1024]{0,1:T(8,128)(2,1)S(1)} %bitcast.239), kind=kOutput, calls=%fused_computation.22 | convolution fusion | flops 4452252672 | bytes 27271168 | tf_op jit(solution)/shard_map/gd,fd->gf/dot_general | solution.py:564
  273.3 5.8 %convolution_convert_fusion.5 = bf16[1024,1024]{0,1:T(8,128)(2,1)} fusion(bf16[2048,1024]{1,0:T(8,128)(2,1)S(1)} %copy-done.16, bf16[2048,1024]{1,0:T(8,128)(2,1)S(1)} %get-tuple-element.156), kind=kOutput, calls=%fused_computation.136 | convolution fusion | flops 4296015872 | bytes 10485760 | tf_op jit(solution)/shard_map/gd,gf->df/dot_general | solution.py:628
  279.1 10.1 %multiply_convert_fusion.3 = bf16[2048,1024]{1,0:T(8,128)(2,1)} fusion(f32[2048,1024]{1,0:T(8,128)} %get-tuple-element.157, f32[2048,1024]{1,0:T(8,128)} %copy-done.11, f32[1024]{0:T(1024)S(1)} %dynamic_slice.15), kind=kLoop, calls=%fused_computation.28 | loop fusion | flops 8388608 | bytes 20975616 | tf_op jit(solution)/shard_map/convert_element_type | solution.py:557
  290.4 9.4 %convolution_convert_fusion.3 = bf16[2048,1024]{1,0:T(8,128)(2,1)} fusion(bf16[2048,1024]{1,0:T(8,128)(2,1)} %copy-done.52, bf16[1024,1792]{1,0:T(8,128)(2,1)} %bitcast.264), kind=kOutput, calls=%fused_computation.70 | convolution fusion | flops 4297064448 | bytes 10485760 | tf_op jit(solution)/shard_map/gf,df->gd/dot_general | solution.py:632
  312.8 6.1 %multiply_reduce_fusion.1 = (f32[4,512]{1,0:T(4,128)S(1)}, f32[4,512,1536]{2,1,0:T(8,128)}) fusion(f32[4,512,1536]{2,1,0:T(8,128)S(1)} %get-tuple-element.225, f32[4,512]{1,0:T(4,128)S(1)} %log_add_fusion.1, bf16[512,4,64]{0,2,1:T(8,128)(2,1)S(1)} %bitcast.232, bf16[1536,4,64]{0,2,1:T(8,128)(2,1)S(1)} %bitcast.228), kind=kOutput, calls=%fused_computation.10 | convolution fusion | flops 412088320 | bytes 26230784 | tf_op jit(solution)/shard_map/qhd,khd->hqk/dot_general | solution.py:589
  318.8 6.6 %multiply_convert_fusion.1 = bf16[4,512,1536]{2,1,0:T(8,128)(2,1)S(1)} fusion(f32[4,512,1536]{2,1,0:T(8,128)} %get-tuple-element.231, f32[4,512,1536]{2,1,0:T(8,128)S(1)} %get-tuple-element.225, f32[4,512]{1,0:T(4,128)S(1)} %get-tuple-element.230, f32[4,512]{1,0:T(4,128)S(1)} %log_add_fusion.1), kind=kLoop, calls=%fused_computation.9 | loop fusion | flops 12582912 | bytes 31473664 | tf_op jit(solution)/shard_map/convert_element_type | solution.py:593
  328.7 7.5 %fusion.152 = (f32[4,512]{1,0:T(4,128)S(1)}, f32[4,512,2048]{2,1,0:T(8,128)}) fusion(bf16[512,4,64]{0,2,1:T(8,128)(2,1)S(1)} %copy-done.32, bf16[2048,4,16]{0,2,1:T(8,128)(2,1)S(1)} %get-tuple-element.188, bf16[2048,4,48]{0,2,1:T(8,128)(2,1)S(1)} %slice.675, pred[512,2048]{1,0:T(8,128)(4,1)S(1)} %copy-done.34), kind=kOutput, calls=%fused_computation.268 | convolution fusion | flops 551548928 | bytes 19144704 | tf_op jit(solution)/shard_map/qhd,khd->hqk/dot_general | solution.py:534
  336.2 8.2 %fusion = f32[4,512]{1,0:T(4,128)S(1)} fusion(f32[4,512,2048]{2,1,0:T(8,128)} %get-tuple-element.227, f32[4,512]{1,0:T(4,128)S(1)} %get-tuple-element.226), kind=kLoop, calls=%fused_computation.6 | loop fusion | flops 8386560 | bytes 16793600 | tf_op jit(solution)/shard_map/reduce_sum | solution.py:545
  344.4 9.2 %convert_reduce_fusion.6 = (f32[4,64]{1,0:T(4,128)S(1)}, bf16[2048,4,64]{0,2,1:T(8,128)(2,1)}) fusion(f32[2048,4,64]{0,2,1:T(8,128)} %fusion.48, bf16[512,4,64]{0,2,1:T(8,128)(2,1)S(1)} %bitcast.225, f32[4,512,2048]{2,1,0:T(8,128)} %get-tuple-element.227, f32[4,512]{1,0:T(4,128)S(1)} %log_add_fusion), kind=kOutput, calls=%fused_computation.128 | convolution fusion | flops 547356416 | bytes 20194304 | tf_op jit(solution)/shard_map/hqk,qhd->khd/dot_general | solution.py:608
  353.9 7.6 %fusion.109 = bf16[512,4,64]{0,2,1:T(8,128)(2,1)S(1)} fusion(bf16[2048,4,64]{0,2,1:T(8,128)(2,1)S(1)} %bitcast.208, f32[4,512,2048]{2,1,0:T(8,128)} %get-tuple-element.227, f32[4,512]{1,0:T(4,128)S(1)} %fusion, f32[4,512]{1,0:T(4,128)S(1)} %get-tuple-element.226), kind=kOutput, calls=%fused_computation.176 | convolution fusion | flops 549584896 | bytes 18104320 | tf_op jit(solution)/shard_map/hqk,khd->qhd/dot_general | solution.py:548
  364.9 10.7 %convolution_convert_fusion = bf16[1280,1024]{0,1:T(8,128)(2,1)} fusion(bf16[2048,1024]{1,0:T(8,128)(2,1)} %bitcast.261, bf16[2048,1024]{1,0:T(8,128)(2,1)} %multiply_convert_fusion.3, bf16[2048,256]{1,0:T(8,128)(2,1)} %copy.55), kind=kOutput, calls=%fused_computation.67 | convolution fusion | flops 5380505600 | bytes 12058624 | tf_op jit(solution)/shard_map/gf,gd->fd/dot_general | solution.py:560
  375.6 7.6 %convolution_convert_fusion.1 = bf16[2048,1024]{1,0:T(8,128)(2,1)} fusion(bf16[1280,1024]{0,1:T(8,128)(2,1)S(1)} %bitcast.229, bf16[2048,1024]{1,0:T(8,128)(2,1)S(1)} %copy-done.19, bf16[2048,256]{1,0:T(8,128)(2,1)S(1)} %copy-done.35), kind=kOutput, calls=%fused_computation.68 | convolution fusion | flops 5381292032 | bytes 12058624 | tf_op jit(solution)/shard_map/dot_general | solution.py:559
  387.6 15.2 %multiply_reduce_fusion = (f32[4,512]{1,0:T(4,128)S(1)}, f32[4,512,2048]{2,1,0:T(8,128)}) fusion(f32[4,512,2048]{2,1,0:T(8,128)} %get-tuple-element.227, f32[4,512]{1,0:T(4,128)S(1)} %log_add_fusion, bf16[512,4,64]{0,2,1:T(8,128)(2,1)S(1)} %bitcast.226, bf16[2048,4,64]{0,2,1:T(8,128)(2,1)S(1)} %bitcast.209), kind=kOutput, calls=%fused_computation.1 | convolution fusion | flops 549451776 | bytes 34881536 | tf_op jit(solution)/shard_map/qhd,khd->hqk/dot_general | solution.py:589
  404.0 10.5 %multiply_convert_fusion = bf16[4,512,2048]{2,1,0:T(8,128)(2,1)} fusion(f32[4,512,2048]{2,1,0:T(8,128)} %get-tuple-element.229, f32[4,512,2048]{2,1,0:T(8,128)S(1)} %bitcast.207, f32[4,512]{1,0:T(4,128)S(1)} %get-tuple-element.228, f32[4,512]{1,0:T(4,128)S(1)} %log_add_fusion), kind=kLoop, calls=%fused_computation | loop fusion | flops 16777216 | bytes 41959424 | tf_op jit(solution)/shard_map/convert_element_type | solution.py:593
  414.5 6.2 %fusion.98 = f32[512,4,64]{0,2,1:T(8,128)S(1)} fusion(bf16[4,512,2048]{2,1,0:T(8,128)(2,1)} %multiply_convert_fusion, bf16[2048,4,16]{0,2,1:T(8,128)(2,1)S(1)} %get-tuple-element.188, bf16[2048,4,48]{0,2,1:T(8,128)(2,1)S(1)} %slice.675), kind=kOutput, calls=%fused_computation.165 | convolution fusion | flops 539099136 | bytes 9961472 | tf_op jit(solution)/shard_map/hqk,khd->qhd/dot_general | solution.py:595
  428.3 5.6 convolution_convert_fusion.6
  433.9 5.3 convolution_convert_fusion.2
  439.3 5.5 pad_maximum_fusion.parts
  446.9 6.0 %copy.62 = bf16[1024,1792]{1,0:T(8,128)(2,1)} copy(bf16[1024,1792]{0,1:T(8,128)(2,1)} %pad_maximum_fusion.2) | data formatting | bytes 7340032 | tf_op jit(solution)/shard_map/concatenate | solution.py:635
  452.9 84.5 %shard_map.333 = (bf16[3,512,1024]{2,1,0:T(8,128)(2,1)}, f32[128,1792]{1,0:T(8,128)}, f32[1280,128]{1,0:T(8,128)}) custom-call(bf16[3,4,512,1024]{3,2,1,0:T(8,128)(2,1)} %pad_maximum_fusion.parts, bf16[8,128,1792]{2,1,0:T(8,128)(2,1)} %bitcast.210, bf16[8,1280,128]{2,1,0:T(8,128)(2,1)} %bitcast.211), custom_call_target="tpu_custom_call" | custom-call | tf_op jit(solution)/shard_map/pallas_call | solution.py:347
  549.4 10.6 %shard_map.334 = f32[8,128]{1,0:T(8,128)} custom-call(f32[4,8,8,128]{3,2,1,0:T(8,128)} %bitcast.252), custom_call_target="tpu_custom_call" | custom-call | tf_op jit(solution)/shard_map/pallas_call | solution.py:410
  (260 shorter events, 133.5 us)
Async XLA Ops:
  6.9 198.3 %copy-start.27 = (f32[2048,16]{0,1:T(8,128)}, f32[2048,16]{0,1:T(8,128)S(1)}, u32[]{:S(2)}) copy-start(f32[2048,16]{0,1:T(8,128)S(1)} %get-tuple-element.238) | copy-start | bytes 393220
  175.4 15.3 %copy-start.40 = (f32[1024]{0:T(1024)}, f32[1024]{0:T(1024)S(1)}, u32[]{:S(2)}) copy-start(f32[1024]{0:T(1024)S(1)} %mul.350) | copy-start | bytes 12292
  175.5 15.3 %copy-start.42 = (f32[1024]{0:T(1024)}, f32[1024]{0:T(1024)S(1)}, u32[]{:S(2)}) copy-start(f32[1024]{0:T(1024)S(1)} %mul.333) | copy-start | bytes 12292
  239.6 8.0 %copy-start.4 = (f32[2048,4,64]{0,2,1:T(8,128)}, f32[2048,4,64]{0,2,1:T(8,128)S(1)}, u32[]{:S(2)}) copy-start(f32[2048,4,64]{0,2,1:T(8,128)S(1)} %fusion.88) | copy-start | bytes 6291460
  247.7 25.7 %copy-start.11 = (f32[2048,1024]{1,0:T(8,128)}, f32[2048,1024]{1,0:T(8,128)S(1)}, u32[]{:S(2)}) copy-start(f32[2048,1024]{1,0:T(8,128)S(1)} %fusion.78) | copy-start | bytes 25165828
  290.4 9.4 %copy-start.36 = (pred[512,1536]{1,0:T(8,128)(4,1)S(1)}, pred[512,1536]{1,0:T(8,128)(4,1)}, u32[]{:S(2)}) copy-start(pred[512,1536]{1,0:T(8,128)(4,1)} %compare_and_fusion) | copy-start | bytes 2359300
  326.7 9.6 %copy-start.6 = (f32[2048,4,64]{0,2,1:T(8,128)}, f32[2048,4,64]{0,2,1:T(8,128)S(1)}, u32[]{:S(2)}) copy-start(f32[2048,4,64]{0,2,1:T(8,128)S(1)} %fusion.36) | copy-start | bytes 6291460
  336.2 8.2 %copy-start.20 = (bf16[512,256]{0,1:T(8,128)(2,1)S(1)}, bf16[512,256]{0,1:T(8,128)(2,1)}, u32[]{:S(2)}) copy-start(bf16[512,256]{0,1:T(8,128)(2,1)} %get-tuple-element.176) | copy-start | bytes 786436
  344.4 9.5 %copy-start.9 = (bf16[2048,256]{0,1:T(8,128)(2,1)S(1)}, bf16[2048,256]{0,1:T(8,128)(2,1)}, u32[]{:S(2)}) copy-start(bf16[2048,256]{0,1:T(8,128)(2,1)} %copy-done.8) | copy-start | bytes 3145732
  353.9 7.6 %copy-start.37 = (bf16[512,4,64]{0,2,1:T(8,128)(2,1)S(1)}, bf16[512,4,64]{0,2,1:T(8,128)(2,1)}, u32[]{:S(2)}) copy-start(bf16[512,4,64]{0,2,1:T(8,128)(2,1)} %fusion.112) | copy-start | bytes 786436
  353.9 7.6 %copy-start.38 = (bf16[512,4,64]{0,2,1:T(8,128)(2,1)S(1)}, bf16[512,4,64]{0,2,1:T(8,128)(2,1)}, u32[]{:S(2)}) copy-start(bf16[512,4,64]{0,2,1:T(8,128)(2,1)} %fusion.111) | copy-start | bytes 786436
  353.9 7.6 %copy-start.39 = (bf16[512,4,64]{0,2,1:T(8,128)(2,1)S(1)}, bf16[512,4,64]{0,2,1:T(8,128)(2,1)}, u32[]{:S(2)}) copy-start(bf16[512,4,64]{0,2,1:T(8,128)(2,1)} %fusion.110) | copy-start | bytes 786436
  364.9 10.7 %copy-start.19 = (bf16[2048,1024]{1,0:T(8,128)(2,1)S(1)}, bf16[2048,1024]{1,0:T(8,128)(2,1)}, u32[]{:S(2)}) copy-start(bf16[2048,1024]{1,0:T(8,128)(2,1)} %multiply_convert_fusion.3) | copy-start | bytes 12582916
  364.9 10.7 %copy-start.22 = (bf16[1280,8,128]{0,2,1:T(8,128)(2,1)S(1)}, bf16[1280,8,128]{0,2,1:T(8,128)(2,1)}, u32[]{:S(2)}) copy-start(bf16[1280,8,128]{0,2,1:T(8,128)(2,1)} %copy.56) | copy-start | bytes 7864324
  364.9 10.7 %copy-start.35 = (bf16[2048,256]{1,0:T(8,128)(2,1)S(1)}, bf16[2048,256]{1,0:T(8,128)(2,1)}, u32[]{:S(2)}) copy-start(bf16[2048,256]{1,0:T(8,128)(2,1)} %copy.55) | copy-start | bytes 3145732
  387.6 15.2 %slice-start = ((s8[16777216]{0:T(1024)(128)(4,1)}), s8[4194304]{0:T(1024)(128)(4,1)S(1)}, s32[]{:S(2)}) async-start(s8[16777216]{0:T(1024)(128)(4,1)} %bitcast.206), calls=%async_computation | async-start | bytes 8388608
  387.6 15.2 %slice-start.1 = ((s8[16777216]{0:T(1024)(128)(4,1)}), s8[4194304]{0:T(1024)(128)(4,1)S(1)}, s32[]{:S(2)}) async-start(s8[16777216]{0:T(1024)(128)(4,1)} %bitcast.206), calls=%async_computation.1 | async-start | bytes 8388608
  387.6 15.2 %slice-start.2 = ((s8[16777216]{0:T(1024)(128)(4,1)}), s8[4194304]{0:T(1024)(128)(4,1)S(1)}, s32[]{:S(2)}) async-start(s8[16777216]{0:T(1024)(128)(4,1)} %bitcast.206), calls=%async_computation.2 | async-start | bytes 8388608
  387.6 16.4 %slice-start.3 = ((s8[16777216]{0:T(1024)(128)(4,1)}), s8[4194304]{0:T(1024)(128)(4,1)S(1)}, s32[]{:S(2)}) async-start(s8[16777216]{0:T(1024)(128)(4,1)} %bitcast.206), calls=%async_computation.3 | async-start | bytes 8388608
  452.9 84.5 %copy-start.3 = (bf16[512,1024]{1,0:T(8,128)(2,1)S(1)}, bf16[512,1024]{1,0:T(8,128)(2,1)}, u32[]{:S(2)}) copy-start(bf16[512,1024]{1,0:T(8,128)(2,1)} %tok.1) | copy-start | bytes 3145732
  452.9 84.5 %copy-start.41 = (f32[1024]{0:T(1024)S(1)}, f32[1024]{0:T(1024)}, u32[]{:S(2)}) copy-start(f32[1024]{0:T(1024)} %copy-done.40) | copy-start | bytes 12292
  452.9 84.5 %copy-start.43 = (f32[1024]{0:T(1024)S(1)}, f32[1024]{0:T(1024)}, u32[]{:S(2)}) copy-start(f32[1024]{0:T(1024)} %copy-done.42) | copy-start | bytes 12292
  452.9 84.5 %copy-start.46 = (f32[512]{0:T(512)S(1)}, f32[512]{0:T(512)}, u32[]{:S(2)}) copy-start(f32[512]{0:T(512)} %broadcast_multiply_fusion.2) | copy-start | bytes 6148
  562.8 7.6 %copy-start.49 = (f32[32]{0:T(128)}, f32[32]{0:T(128)S(1)}, u32[]{:S(2)}) copy-start(f32[32]{0:T(128)S(1)} %get-tuple-element.278) | copy-start | bytes 388
  (34 other events, 120.4 us)

commit v2 on v1

--- a/solution.py
+++ b/solution.py
@@ -25,8 +25,10 @@
     return centred * lax.rsqrt(row_var + EPS) * gain_vec + shift_vec
 
 
-def smooth(values):
-    return jax.nn.gelu(values, approximate=False)
+def smooth_and_slope(values):
+    below = 0.5 * (1.0 + lax.erf(values * math.sqrt(0.5)))
+    density = jnp.exp(-0.5 * values * values) * (1.0 / math.sqrt(2.0 * math.pi))
+    return (values * below, below + values * density)
 
 
 def segment_rows(lengths, group_size):
@@ -204,7 +206,7 @@
 
 
 def gather_all(tok, cot, small, w_in, w_out):
-    anywhere = pl.BlockSpec(memory_space=pl.ANY)
+    inside = pl.BlockSpec(memory_space=pltpu.VMEM)
     shape = jax.ShapeDtypeStruct
     dma = pltpu.SemaphoreType.DMA
     return pl.pallas_call(
@@ -216,8 +218,8 @@
             shape((RING,) + w_in.shape, w_in.dtype),
             shape((RING,) + w_out.shape, w_out.dtype),
         ),
-        in_specs=[anywhere] * 5,
-        out_specs=(anywhere,) * 5,
+        in_specs=[inside] * 5,
+        out_specs=(inside,) * 5,
         scratch_shapes=[
             dma((5,)),
             dma((3, 2)),
@@ -229,7 +231,9 @@
             dma((RING - 1,)),
             dma((RING - 1,)),
         ],
-        compiler_params=pltpu.CompilerParams(collective_id=0, has_side_effects=True),
+        compiler_params=pltpu.CompilerParams(
+            collective_id=0, has_side_effects=True, vmem_limit_bytes=VMEM_BYTES
+        ),
     )(tok, cot, small, w_in, w_out)
 
 
@@ -554,7 +558,8 @@
         jnp.concatenate(context_parts, 0).reshape(group_size, column_count).astype(jnp.bfloat16)
     )
     hidden_pre = up_raw + bias_up
-    activated = smooth(hidden_pre).astype(jnp.bfloat16)
+    activated, slope = smooth_and_slope(hidden_pre)
+    activated, slope = lax.optimization_barrier((activated.astype(jnp.bfloat16), slope))
     joined = jnp.concatenate([context, activated], 1)
     partial_cols = jnp.dot(joined, w_out, preferred_element_type=jnp.float32).astype(jnp.bfloat16)
     grad_out = jnp.einsum("gf,gd->fd", joined, grad_group, preferred_element_type=jnp.float32)
@@ -565,8 +570,7 @@
         "gd,fd->gf", grad_group, w_out[column_count:], preferred_element_type=jnp.float32
     )
     grad_context = grad_context.astype(jnp.bfloat16).reshape(group_size, heads_here, HEAD)
-    gelu_value, gelu_back = jax.vjp(smooth, hidden_pre)
-    grad_hidden = gelu_back(grad_act)[0].astype(jnp.bfloat16)
+    grad_hidden = (grad_act * slope).astype(jnp.bfloat16)
     query_parts = []
     key_total = jnp.zeros((group_size, heads_here, HEAD), jnp.float32)
     value_total = jnp.zeros((group_size, heads_here, HEAD), jnp.float32)

time: 579 us -> 470 us (0.81)
  Pallas kernels: 248 us -> 173 us
  other arithmetic: 99.7 us -> 78.6 us
  matrix products: 171 us -> 159 us
    pallas_call x1, Pallas kernels: 153 us -> 77.8 us  [gather_all(): pl.pallas_call(gather_kernel, out_shape=(shape((4,) + tok.shape, tok.dtyp...]
    dot_general x1, matrix products: 25.6 us -> 6.06 us  [per_device(): jnp.einsum('gd,fd->gf', grad_group, w_out[column_count:], preferred_eleme...]
    reduce_sum x4, other arithmetic: 23.7 us -> 12.9 us  [per_device(): row_total = jnp.sum(expd, axis=-1, keepdims=True)]
    convert_element_type x1 -> x0, other arithmetic: 10.1 us -> none  [per_device(): activated = smooth(hidden_pre).astype(jnp.bfloat16)]
    dot_general x1, matrix products: 4.54 us -> 12.9 us  [per_device(): up_raw = jnp.dot(normed_two, w_hidden, preferred_element_type=jnp.float32)]
where the time goes in v2:
time: 470 us; the launch traced here: 462 us
  Pallas kernels  173 us (37%)
  matrix products  159 us (34%)
  other arithmetic  78.6 us (17%)
  local copies, waits for them, and re-layouts  49.8 us (11%)
    pallas_call x1, Pallas kernels, scatter_all(): pl.pallas_call(scatter_kernel, out_shape=(shape((count, rows, width), jnp...  84.4 us
    pallas_call x1, Pallas kernels, gather_all(): pl.pallas_call(gather_kernel, out_shape=(shape((4,) + tok.shape, tok.dtyp...  77.8 us
    dot_general x4, matrix products, per_device(): jnp.einsum('qhd,khd->hqk', grad_blk, values[:high_row], preferred_element...  24.9 us
    convert_element_type x4, other arithmetic, per_device(): grad_scores = (probs_full * (grad_probs - row_inner)).astype(jnp.bfloat16)  19.8 us
    dot_general x4, matrix products, per_device(): jnp.einsum('hqk,qhd->khd', probs_full.astype(jnp.bfloat16), grad_blk, pre...  16.1 us
    dot_general x4, matrix products, per_device(): jnp.einsum('hqk,khd->qhd', attn_probs, values[:high_row], preferred_eleme...  15.9 us
    dot_general x1, matrix products, per_device(): up_raw = jnp.dot(normed_two, w_hidden, preferred_element_type=jnp.float32)  12.9 us
    reduce_sum x4, other arithmetic, per_device(): row_total = jnp.sum(expd, axis=-1, keepdims=True)  12.9 us

profile of v2, /device:TPU:0, one launch (start us, length us, event | category | flops | bytes accessed | tf_op | source)
XLA Modules:
  0.0 462.3 jit_solution(8091058409703073954)
XLA Ops:
  16.4 77.8 %shard_map.332 = (bf16[4,512,1024]{2,1,0:T(8,128)(2,1)}, bf16[4,512,1024]{2,1,0:T(8,128)(2,1)}, f32[8,4,8,128]{3,2,1,0:T(8,128)}, bf16[8,128,1792]{2,1,0:T(8,128)(2,1)}, bf16[8,1280,128]{2,1,0:T(8,128)(2,1)}) custom-call(bf16[512,1024]{1,0:T(8,128)(2,1)} %tok.1, bf16[512,1024]{1,0:T(8,128)(2,1)} %cot.1, f32[8,128]{1,0:T(8,128)} %pad_bitcast_fusion.1.small, ...), custom_call_target="tpu_custom_call" | custom-call | tf_op jit(solution)/shard_map/pallas_call | solution.py:212
  115.5 5.5 %add_convert_fusion.1 = (bf16[2048,1024]{1,0:T(8,128)(2,1)S(1)}, bf16[2048,1024]{1,0:T(8,128)(2,1)}) fusion(bf16[4,512,1024]{2,1,0:T(8,128)(2,1)} %get-tuple-element.140, f32[1024]{0:T(1024)S(1)} %add.246, f32[1024]{0:T(1024)S(1)} %mul.337, f32[2048]{0:T(1024)S(1)} %bitcast.257, f32[2048]{0:T(1024)S(1)} %bitcast.256, f32[1024]{0:T(1024)S(1)} %add.258, ...), kind=kLoop, calls=%fused_computation.37 | loop fusion | flops 18874368 | bytes 12615680 | tf_op jit(solution)/shard_map/convert_element_type | solution.py:507
  123.1 5.0 %fusion.79 = f32[2048,768]{0,1:T(8,128)S(1)} fusion(bf16[2048,1024]{1,0:T(8,128)(2,1)S(1)} %get-tuple-element.170, bf16[1024,1792]{1,0:T(8,128)(2,1)} %bitcast.263), kind=kOutput, calls=%fused_computation.141 | convolution fusion | flops 3221225472 | bytes 12058624 | tf_op jit(solution)/shard_map/dot_general | solution.py:515
  169.5 6.2 %multiply_reduce_fusion.1 = (f32[4,512]{1,0:T(4,128)S(1)}, f32[4,512,1536]{2,1,0:T(8,128)}) fusion(f32[4,512,1536]{2,1,0:T(8,128)S(1)} %get-tuple-element.228, f32[4,512]{1,0:T(4,128)S(1)} %log_add_fusion.1, bf16[512,4,64]{0,2,1:T(8,128)(2,1)S(1)} %bitcast.232, bf16[1536,4,64]{0,2,1:T(8,128)(2,1)S(1)} %bitcast.228), kind=kOutput, calls=%fused_computation.10 | convolution fusion | flops 412088320 | bytes 26230784 | tf_op jit(solution)/shard_map/qhd,khd->hqk/dot_general | solution.py:593
  175.8 6.4 %multiply_convert_fusion.1 = bf16[4,512,1536]{2,1,0:T(8,128)(2,1)S(1)} fusion(f32[4,512,1536]{2,1,0:T(8,128)} %get-tuple-element.234, f32[4,512,1536]{2,1,0:T(8,128)S(1)} %get-tuple-element.228, f32[4,512]{1,0:T(4,128)S(1)} %get-tuple-element.233, f32[4,512]{1,0:T(4,128)S(1)} %log_add_fusion.1), kind=kLoop, calls=%fused_computation.9 | loop fusion | flops 12582912 | bytes 31473664 | tf_op jit(solution)/shard_map/convert_element_type | solution.py:597
  186.6 12.9 %fusion.7 = (f32[2048,1024]{1,0:T(8,128)S(1)}, bf16[2048,1024]{1,0:T(8,128)(2,1)}) fusion(f32[1024]{0:T(1024)S(1)} %dynamic-slice-done, bf16[2048,1024]{1,0:T(8,128)(2,1)S(1)} %copy-done.15, bf16[1024,1792]{1,0:T(8,128)(2,1)S(1)} %bitcast.265), kind=kOutput, calls=%fused_computation.21 | convolution fusion | flops 4318035968 | bytes 18878464 | tf_op jit(solution)/shard_map/dot_general | solution.py:519
  199.5 6.1 %convert_reduce_fusion = (f32[1024]{0:T(1024)S(1)}, bf16[2048,1024]{1,0:T(8,128)(2,1)}) fusion(f32[2048,1024]{1,0:T(8,128)S(1)} %get-tuple-element.146, bf16[2048,1024]{1,0:T(8,128)(2,1)S(1)} %bitcast.262, bf16[1024,1024]{0,1:T(8,128)(2,1)S(1)} %bitcast.239), kind=kOutput, calls=%fused_computation.25 | convolution fusion | flops 4303354880 | bytes 18878464 | tf_op jit(solution)/shard_map/gd,fd->gf/dot_general | solution.py:569
  205.6 8.2 %convolution_convert_fusion.5 = bf16[1024,1024]{0,1:T(8,128)(2,1)} fusion(bf16[2048,1024]{1,0:T(8,128)(2,1)S(1)} %copy-done.15, bf16[2048,1024]{1,0:T(8,128)(2,1)} %get-tuple-element.242), kind=kOutput, calls=%fused_computation.127 | convolution fusion | flops 4296015872 | bytes 10485760 | tf_op jit(solution)/shard_map/gd,gf->df/dot_general | solution.py:632
  214.0 6.6 %convolution_convert_fusion.3 = bf16[2048,1024]{1,0:T(8,128)(2,1)} fusion(bf16[2048,1024]{1,0:T(8,128)(2,1)S(1)} %copy-done.48, bf16[1024,1792]{1,0:T(8,128)(2,1)S(1)} %bitcast.266), kind=kOutput, calls=%fused_computation.61 | convolution fusion | flops 4297064448 | bytes 10485760 | tf_op jit(solution)/shard_map/gf,df->gd/dot_general | solution.py:636
  220.6 7.5 %fusion.149 = (f32[4,512]{1,0:T(4,128)S(1)}, f32[4,512,2048]{2,1,0:T(8,128)}) fusion(bf16[512,4,64]{0,2,1:T(8,128)(2,1)S(1)} %copy-done.29, bf16[2048,4,16]{0,2,1:T(8,128)(2,1)S(1)} %get-tuple-element.191, bf16[2048,4,48]{0,2,1:T(8,128)(2,1)S(1)} %slice.675, pred[512,2048]{1,0:T(8,128)(4,1)S(1)} %copy-done.31), kind=kOutput, calls=%fused_computation.259 | convolution fusion | flops 551548928 | bytes 19144704 | tf_op jit(solution)/shard_map/qhd,khd->hqk/dot_general | solution.py:538
  228.1 8.2 %fusion = f32[4,512]{1,0:T(4,128)S(1)} fusion(f32[4,512,2048]{2,1,0:T(8,128)} %get-tuple-element.230, f32[4,512]{1,0:T(4,128)S(1)} %get-tuple-element.229), kind=kLoop, calls=%fused_computation.6 | loop fusion | flops 8386560 | bytes 16793600 | tf_op jit(solution)/shard_map/reduce_sum | solution.py:549
  236.3 9.2 %convert_reduce_fusion.6 = (f32[4,64]{1,0:T(4,128)S(1)}, bf16[2048,4,64]{0,2,1:T(8,128)(2,1)}) fusion(f32[2048,4,64]{0,2,1:T(8,128)} %fusion.46, bf16[512,4,64]{0,2,1:T(8,128)(2,1)S(1)} %bitcast.225, f32[4,512,2048]{2,1,0:T(8,128)} %get-tuple-element.230, f32[4,512]{1,0:T(4,128)S(1)} %log_add_fusion), kind=kOutput, calls=%fused_computation.119 | convolution fusion | flops 547356416 | bytes 20194304 | tf_op jit(solution)/shard_map/hqk,qhd->khd/dot_general | solution.py:612
  245.8 7.6 %fusion.107 = bf16[512,4,64]{0,2,1:T(8,128)(2,1)S(1)} fusion(bf16[2048,4,64]{0,2,1:T(8,128)(2,1)S(1)} %bitcast.208, f32[4,512,2048]{2,1,0:T(8,128)} %get-tuple-element.230, f32[4,512]{1,0:T(4,128)S(1)} %fusion, f32[4,512]{1,0:T(4,128)S(1)} %get-tuple-element.229), kind=kOutput, calls=%fused_computation.167 | convolution fusion | flops 549584896 | bytes 18104320 | tf_op jit(solution)/shard_map/hqk,khd->qhd/dot_general | solution.py:552
  256.8 10.7 %convolution_convert_fusion = bf16[1280,1024]{0,1:T(8,128)(2,1)} fusion(bf16[2048,1024]{1,0:T(8,128)(2,1)} %bitcast.261, bf16[2048,1024]{1,0:T(8,128)(2,1)} %get-tuple-element.143, bf16[2048,256]{1,0:T(8,128)(2,1)} %copy.55), kind=kOutput, calls=%fused_computation.58 | convolution fusion | flops 5380505600 | bytes 12058624 | tf_op jit(solution)/shard_map/gf,gd->fd/dot_general | solution.py:565
  267.4 7.6 %convolution_convert_fusion.1 = bf16[2048,1024]{1,0:T(8,128)(2,1)} fusion(bf16[1280,1024]{0,1:T(8,128)(2,1)S(1)} %bitcast.229, bf16[2048,1024]{1,0:T(8,128)(2,1)S(1)} %copy-done.49, bf16[2048,256]{1,0:T(8,128)(2,1)S(1)} %copy-done.32), kind=kOutput, calls=%fused_computation.59 | convolution fusion | flops 5381292032 | bytes 12058624 | tf_op jit(solution)/shard_map/dot_general | solution.py:564
  279.5 15.2 %multiply_reduce_fusion = (f32[4,512]{1,0:T(4,128)S(1)}, f32[4,512,2048]{2,1,0:T(8,128)}) fusion(f32[4,512,2048]{2,1,0:T(8,128)} %get-tuple-element.230, f32[4,512]{1,0:T(4,128)S(1)} %log_add_fusion, bf16[512,4,64]{0,2,1:T(8,128)(2,1)S(1)} %bitcast.226, bf16[2048,4,64]{0,2,1:T(8,128)(2,1)S(1)} %bitcast.209), kind=kOutput, calls=%fused_computation.1 | convolution fusion | flops 549451776 | bytes 34881536 | tf_op jit(solution)/shard_map/qhd,khd->hqk/dot_general | solution.py:593
  295.9 10.4 %multiply_convert_fusion = bf16[4,512,2048]{2,1,0:T(8,128)(2,1)} fusion(f32[4,512,2048]{2,1,0:T(8,128)} %get-tuple-element.232, f32[4,512,2048]{2,1,0:T(8,128)S(1)} %bitcast.207, f32[4,512]{1,0:T(4,128)S(1)} %get-tuple-element.231, f32[4,512]{1,0:T(4,128)S(1)} %log_add_fusion), kind=kLoop, calls=%fused_computation | loop fusion | flops 16777216 | bytes 41959424 | tf_op jit(solution)/shard_map/convert_element_type | solution.py:597
  306.3 6.2 %fusion.96 = f32[512,4,64]{0,2,1:T(8,128)S(1)} fusion(bf16[4,512,2048]{2,1,0:T(8,128)(2,1)} %multiply_convert_fusion, bf16[2048,4,16]{0,2,1:T(8,128)(2,1)S(1)} %get-tuple-element.191, bf16[2048,4,48]{0,2,1:T(8,128)(2,1)S(1)} %slice.675), kind=kOutput, calls=%fused_computation.156 | convolution fusion | flops 539099136 | bytes 9961472 | tf_op jit(solution)/shard_map/hqk,khd->qhd/dot_general | solution.py:599
  320.1 5.6 %convolution_convert_fusion.6 = bf16[1024,768]{0,1:T(8,128)(2,1)S(1)} fusion(bf16[2048,1024]{1,0:T(8,128)(2,1)} %copy-done.14, bf16[2048,256]{0,1:T(8,128)(2,1)S(1)} %bitcast.240, bf16[2048,256]{0,1:T(8,128)(2,1)S(1)} %bitcast.244, bf16[2048,256]{0,1:T(8,128)(2,1)S(1)} %bitcast.246), kind=kOutput, calls=%fused_computation.131 | convolution fusion | flops 3231449088 | bytes 8912896 | tf_op jit(solution)/shard_map/gd,gc->dc/dot_general | solution.py:631
  325.7 5.3 %convolution_convert_fusion.2 = bf16[2048,1024]{1,0:T(8,128)(2,1)S(1)} fusion(bf16[1024,1792]{1,0:T(8,128)(2,1)} %bitcast.264, bf16[2048,256]{0,1:T(8,128)(2,1)S(1)} %bitcast.241, bf16[2048,256]{0,1:T(8,128)(2,1)S(1)} %bitcast.245, bf16[2048,256]{0,1:T(8,128)(2,1)S(1)} %bitcast.247), kind=kOutput, calls=%fused_computation.60 | convolution fusion | flops 3232759808 | bytes 8912896 | tf_op jit(solution)/shard_map/gc,dc->gd/dot_general | solution.py:633
  331.0 5.5 %pad_maximum_fusion.parts = bf16[3,4,512,1024]{3,2,1,0:T(8,128)(2,1)} fusion(bf16[1,4,512,1024]{3,2,1,0:T(8,128)(2,1)S(1)} %bitcast.222, bf16[1,4,512,1024]{3,2,1,0:T(8,128)(2,1)S(1)} %bitcast.224, bf16[1,4,512,1024]{3,2,1,0:T(8,128)(2,1)S(1)} %bitcast.223), kind=kLoop, calls=%fused_computation.8 | loop fusion | flops 12582912 | bytes 25165824 | tf_op jit(solution)/shard_map/stack | solution.py:645
  338.7 6.0 %copy.62 = bf16[1024,1792]{1,0:T(8,128)(2,1)} copy(bf16[1024,1792]{0,1:T(8,128)(2,1)} %pad_maximum_fusion.2) | data formatting | bytes 7340032 | tf_op jit(solution)/shard_map/concatenate | solution.py:639
  344.7 84.4 %shard_map.333 = (bf16[3,512,1024]{2,1,0:T(8,128)(2,1)}, f32[128,1792]{1,0:T(8,128)}, f32[1280,128]{1,0:T(8,128)}) custom-call(bf16[3,4,512,1024]{3,2,1,0:T(8,128)(2,1)} %pad_maximum_fusion.parts, bf16[8,128,1792]{2,1,0:T(8,128)(2,1)} %bitcast.210, bf16[8,1280,128]{2,1,0:T(8,128)(2,1)} %bitcast.211), custom_call_target="tpu_custom_call" | custom-call | tf_op jit(solution)/shard_map/pallas_call | solution.py:351
  441.1 10.6 %shard_map.334 = f32[8,128]{1,0:T(8,128)} custom-call(f32[4,8,8,128]{3,2,1,0:T(8,128)} %bitcast.252), custom_call_target="tpu_custom_call" | custom-call | tf_op jit(solution)/shard_map/pallas_call | solution.py:414
  (254 shorter events, 125.9 us)
Async XLA Ops:
  6.9 122.6 %copy-start.24 = (f32[2048,16]{0,1:T(8,128)}, f32[2048,16]{0,1:T(8,128)S(1)}, u32[]{:S(2)}) copy-start(f32[2048,16]{0,1:T(8,128)S(1)} %get-tuple-element.243) | copy-start | bytes 393220
  100.2 15.3 %copy-start.37 = (f32[1024]{0:T(1024)}, f32[1024]{0:T(1024)S(1)}, u32[]{:S(2)}) copy-start(f32[1024]{0:T(1024)S(1)} %mul.354) | copy-start | bytes 12292
  100.3 15.3 %copy-start.39 = (f32[1024]{0:T(1024)}, f32[1024]{0:T(1024)S(1)}, u32[]{:S(2)}) copy-start(f32[1024]{0:T(1024)S(1)} %mul.337) | copy-start | bytes 12292
  183.5 16.1 %copy-start.6 = (f32[2048,4,64]{0,2,1:T(8,128)}, f32[2048,4,64]{0,2,1:T(8,128)S(1)}, u32[]{:S(2)}) copy-start(f32[2048,4,64]{0,2,1:T(8,128)S(1)} %fusion.34) | copy-start | bytes 6291460
  186.6 12.9 %copy-start.23 = (bf16[1024,8,128]{0,2,1:T(8,128)(2,1)S(1)}, bf16[1024,8,128]{0,2,1:T(8,128)(2,1)}, u32[]{:S(2)}) copy-start(bf16[1024,8,128]{0,2,1:T(8,128)(2,1)} %copy.61) | copy-start | bytes 6291460
  186.6 12.9 %copy-start.46 = (bf16[4,512,1024]{2,1,0:T(8,128)(2,1)S(1)}, bf16[4,512,1024]{2,1,0:T(8,128)(2,1)}, u32[]{:S(2)}) copy-start(bf16[4,512,1024]{2,1,0:T(8,128)(2,1)} %get-tuple-element.145) | copy-start | bytes 12582916
  205.6 8.4 %copy-start.48 = (bf16[2048,1024]{1,0:T(8,128)(2,1)S(1)}, bf16[2048,1024]{1,0:T(8,128)(2,1)}, u32[]{:S(2)}) copy-start(bf16[2048,1024]{1,0:T(8,128)(2,1)} %get-tuple-element.242) | copy-start | bytes 12582916
  228.1 8.2 %copy-start.18 = (bf16[512,256]{0,1:T(8,128)(2,1)S(1)}, bf16[512,256]{0,1:T(8,128)(2,1)}, u32[]{:S(2)}) copy-start(bf16[512,256]{0,1:T(8,128)(2,1)} %get-tuple-element.179) | copy-start | bytes 786436
  236.3 9.5 %copy-start.9 = (bf16[2048,256]{0,1:T(8,128)(2,1)S(1)}, bf16[2048,256]{0,1:T(8,128)(2,1)}, u32[]{:S(2)}) copy-start(bf16[2048,256]{0,1:T(8,128)(2,1)} %copy-done.8) | copy-start | bytes 3145732
  245.8 7.6 %copy-start.34 = (bf16[512,4,64]{0,2,1:T(8,128)(2,1)S(1)}, bf16[512,4,64]{0,2,1:T(8,128)(2,1)}, u32[]{:S(2)}) copy-start(bf16[512,4,64]{0,2,1:T(8,128)(2,1)} %fusion.110) | copy-start | bytes 786436
  245.8 7.6 %copy-start.35 = (bf16[512,4,64]{0,2,1:T(8,128)(2,1)S(1)}, bf16[512,4,64]{0,2,1:T(8,128)(2,1)}, u32[]{:S(2)}) copy-start(bf16[512,4,64]{0,2,1:T(8,128)(2,1)} %fusion.109) | copy-start | bytes 786436
  245.8 7.6 %copy-start.36 = (bf16[512,4,64]{0,2,1:T(8,128)(2,1)S(1)}, bf16[512,4,64]{0,2,1:T(8,128)(2,1)}, u32[]{:S(2)}) copy-start(bf16[512,4,64]{0,2,1:T(8,128)(2,1)} %fusion.108) | copy-start | bytes 786436
  256.8 10.7 %copy-start.19 = (bf16[1280,8,128]{0,2,1:T(8,128)(2,1)S(1)}, bf16[1280,8,128]{0,2,1:T(8,128)(2,1)}, u32[]{:S(2)}) copy-start(bf16[1280,8,128]{0,2,1:T(8,128)(2,1)} %copy.56) | copy-start | bytes 7864324
  256.8 10.7 %copy-start.32 = (bf16[2048,256]{1,0:T(8,128)(2,1)S(1)}, bf16[2048,256]{1,0:T(8,128)(2,1)}, u32[]{:S(2)}) copy-start(bf16[2048,256]{1,0:T(8,128)(2,1)} %copy.55) | copy-start | bytes 3145732
  256.8 10.7 %copy-start.49 = (bf16[2048,1024]{1,0:T(8,128)(2,1)S(1)}, bf16[2048,1024]{1,0:T(8,128)(2,1)}, u32[]{:S(2)}) copy-start(bf16[2048,1024]{1,0:T(8,128)(2,1)} %get-tuple-element.143) | copy-start | bytes 12582916
  279.5 15.2 %slice-start = ((s8[16777216]{0:T(1024)(128)(4,1)}), s8[4194304]{0:T(1024)(128)(4,1)S(1)}, s32[]{:S(2)}) async-start(s8[16777216]{0:T(1024)(128)(4,1)} %bitcast.206), calls=%async_computation | async-start | bytes 8388608
  279.5 15.2 %slice-start.1 = ((s8[16777216]{0:T(1024)(128)(4,1)}), s8[4194304]{0:T(1024)(128)(4,1)S(1)}, s32[]{:S(2)}) async-start(s8[16777216]{0:T(1024)(128)(4,1)} %bitcast.206), calls=%async_computation.1 | async-start | bytes 8388608
  279.5 15.2 %slice-start.2 = ((s8[16777216]{0:T(1024)(128)(4,1)}), s8[4194304]{0:T(1024)(128)(4,1)S(1)}, s32[]{:S(2)}) async-start(s8[16777216]{0:T(1024)(128)(4,1)} %bitcast.206), calls=%async_computation.2 | async-start | bytes 8388608
  279.5 16.4 %slice-start.3 = ((s8[16777216]{0:T(1024)(128)(4,1)}), s8[4194304]{0:T(1024)(128)(4,1)S(1)}, s32[]{:S(2)}) async-start(s8[16777216]{0:T(1024)(128)(4,1)} %bitcast.206), calls=%async_computation.3 | async-start | bytes 8388608
  344.7 84.4 %copy-start.3 = (bf16[512,1024]{1,0:T(8,128)(2,1)S(1)}, bf16[512,1024]{1,0:T(8,128)(2,1)}, u32[]{:S(2)}) copy-start(bf16[512,1024]{1,0:T(8,128)(2,1)} %tok.1) | copy-start | bytes 3145732
  344.7 84.4 %copy-start.38 = (f32[1024]{0:T(1024)S(1)}, f32[1024]{0:T(1024)}, u32[]{:S(2)}) copy-start(f32[1024]{0:T(1024)} %copy-done.37) | copy-start | bytes 12292
  344.7 84.4 %copy-start.40 = (f32[1024]{0:T(1024)S(1)}, f32[1024]{0:T(1024)}, u32[]{:S(2)}) copy-start(f32[1024]{0:T(1024)} %copy-done.39) | copy-start | bytes 12292
  344.7 84.5 %copy-start.41 = (f32[512]{0:T(512)S(1)}, f32[512]{0:T(512)}, u32[]{:S(2)}) copy-start(f32[512]{0:T(512)} %broadcast_multiply_fusion.2) | copy-start | bytes 6148
  454.5 7.6 %copy-start.45 = (f32[32]{0:T(128)}, f32[32]{0:T(128)S(1)}, u32[]{:S(2)}) copy-start(f32[32]{0:T(128)S(1)} %get-tuple-element.283) | copy-start | bytes 388
  (32 other events, 117.5 us)
